TPU v7x, 128 devices: a whole 4x4x4 slice. The times are simulated.
128 devices in a mesh: dp: 16 (over x, y), red: 8 (over z, core).
Axes of the slice: x: 4, y: 4, z: 4, core: 2. Of those that a mesh axis runs over, the one named last changes fastest.
Arguments:
- frames: bfloat16 [2048, 48, 1536], P(('dp', 'red')), may hold values from -36 to 36
- cotangent: bfloat16 [2048, 48, 1536], P(('dp', 'red')), may hold values from -6 to 6
- w_in: bfloat16 [1536, 3072], P('red'), may hold values from -0.15625 to 0.15625
- kernel: float32 [31, 1536], replicated, may hold values from -1 to 1
- gain: float32 [1536], replicated, may hold values from 0.25 to 1.75
- lengths: int32 [2048], replicated, may hold values from 1 to 47, as said below
Outputs:
- module_output: bfloat16 [2048, 48, 1536], P(('dp', 'red'))
- frame_gradient: bfloat16 [2048, 48, 1536], P(('dp', 'red'))
- grad_w_in: float32 [1536, 3072], P('red')
- grad_kernel: float32 [31, 1536], replicated
- grad_gain: float32 [1536], replicated
Inputs may be any that keep to these rules, and one draw needn't show every extreme that they name: The slots of each device, in order, form 16 groups of 1 slots. The q-th slot of group j on the device with dp index i and red index r and the q-th slot of group j on the device with dp index (2 j + 1 - i) mod 16 and the same red index have lengths that sum to exactly 48. The slots of dp index 0 all hold at least three quarters of 48 frames, rounded up.
All inputs are finite; a program needn't handle non-finite values.
Results may differ from a plain program's by a relative error of at most 0.0054.
Values may be sent and summed in bfloat16 or wider, within the bound.
A program may use at most 128 MiB of HBM per device.

v0:
```python
import jax
import jax.numpy as jnp
from jax import lax
from jax.sharding import PartitionSpec as P

EPSILON = 1e-05


def normalize(widened_frames):
    center = widened_frames - jnp.mean(widened_frames, axis=-1, keepdims=True)
    inv_std = lax.rsqrt(jnp.mean(center * center, axis=-1, keepdims=True) + EPSILON)
    return (center * inv_std, inv_std)


def block_pass(frames, cotangent, valid_frame_mask, segment, weights, kernel, gain):
    row_count, length, model_width = frames.shape
    tap_count = kernel.shape[0]
    reach = tap_count // 2
    widened_frames = frames.astype(jnp.float32)
    normed, inv_std = normalize(widened_frames)
    scaled = (normed * gain).astype(jnp.bfloat16)
    flat_in = scaled.reshape(row_count * length, model_width)
    hidden = jnp.dot(flat_in, weights, preferred_element_type=jnp.float32)
    hidden = hidden.reshape(row_count, length, 2 * model_width)
    value_portion = hidden[..., :model_width]
    gate_sigmoid = jax.nn.sigmoid(hidden[..., model_width:])
    frame_validity = valid_frame_mask.astype(jnp.float32)[..., None]
    gated_linear_output = value_portion * gate_sigmoid * frame_validity
    padded = jnp.pad(gated_linear_output, ((0, 0), (reach, reach), (0, 0)))
    seg_pad = jnp.pad(segment, ((0, 0), (reach, reach)), constant_values=-1)
    convolved_frames = jnp.zeros_like(gated_linear_output)
    for offset in range(tap_count):
        window = padded[:, offset : offset + length]
        same_seg = (seg_pad[:, offset : offset + length] == segment).astype(jnp.float32)[..., None]
        convolved_frames = convolved_frames + kernel[offset] * (window * same_seg)
    swish_activation = jax.nn.sigmoid(convolved_frames)
    module_output = (
        (widened_frames + convolved_frames * swish_activation) * frame_validity
    ).astype(jnp.bfloat16)
    incoming_gradient = cotangent.astype(jnp.float32) * frame_validity
    grad_conv = incoming_gradient * (
        swish_activation * (1.0 + convolved_frames * (1.0 - swish_activation))
    )
    grad_pad = jnp.pad(grad_conv, ((0, 0), (reach, reach), (0, 0)))
    gated_linear_gradient = jnp.zeros_like(gated_linear_output)
    kernel_terms = []
    for offset in range(tap_count):
        window = padded[:, offset : offset + length]
        same_seg = (seg_pad[:, offset : offset + length] == segment).astype(jnp.float32)[..., None]
        kernel_terms.append(jnp.sum(grad_conv * window * same_seg, axis=(0, 1)))
        back_start = 2 * reach - offset
        back_same = (seg_pad[:, back_start : back_start + length] == segment).astype(jnp.float32)[
            ..., None
        ]
        gated_linear_gradient = gated_linear_gradient + kernel[offset] * (
            grad_pad[:, back_start : back_start + length] * back_same
        )
    gated_linear_gradient = gated_linear_gradient * frame_validity
    grad_hidden = jnp.concatenate(
        [
            gated_linear_gradient * gate_sigmoid,
            gated_linear_gradient * value_portion * gate_sigmoid * (1.0 - gate_sigmoid),
        ],
        axis=-1,
    ).astype(jnp.bfloat16)
    flat_grad = grad_hidden.reshape(row_count * length, 2 * model_width)
    grad_scaled = lax.dot_general(
        flat_grad, weights, (((1,), (1,)), ((), ())), preferred_element_type=jnp.float32
    )
    grad_scaled = grad_scaled.reshape(row_count, length, model_width)
    gain_term = jnp.sum(grad_scaled * normed, axis=(0, 1))
    grad_normed = grad_scaled * gain
    frame_gradient = incoming_gradient + inv_std * (
        grad_normed
        - jnp.mean(grad_normed, axis=-1, keepdims=True)
        - normed * jnp.mean(grad_normed * normed, axis=-1, keepdims=True)
    )
    frame_gradient = (frame_gradient * frame_validity).astype(jnp.bfloat16)
    return (module_output, frame_gradient, flat_in, flat_grad, jnp.stack(kernel_terms), gain_term)


def local(frames, cotangent, w_in, kernel, gain, lengths):
    dp_size = lax.axis_size("dp")
    red_size = lax.axis_size("red")
    dp_index = lax.axis_index("dp")
    red_index = lax.axis_index("red")
    local_utts, length, model_width = frames.shape
    weights = lax.all_gather(w_in, "red", axis=0, tiled=True)
    positions = jnp.arange(length, dtype=jnp.int32)
    by_owner = lengths.reshape(dp_size, red_size, local_utts)
    own_lengths = lax.dynamic_slice(by_owner, (dp_index, red_index, 0), (1, 1, local_utts)).reshape(
        local_utts
    )
    valid_frame_mask = positions[None, :] < own_lengths[:, None]
    segment = jnp.where(valid_frame_mask, 0, 1).astype(jnp.int32)
    module_output, frame_gradient, flat_in, flat_grad, kernel_part, gain_part = block_pass(
        frames, cotangent, valid_frame_mask, segment, weights, kernel, gain
    )
    grad_scale = lax.rsqrt(jnp.sum(lengths).astype(jnp.float32))
    block_rows = model_width // (dp_size * red_size)
    ordered = flat_in.reshape(-1, red_size, dp_size, block_rows)
    ordered = jnp.transpose(ordered, (0, 2, 1, 3)).reshape(-1, model_width)
    owned_rows = lax.psum_scatter(
        lax.dot_general(
            ordered, flat_grad, (((0,), (0,)), ((), ())), preferred_element_type=jnp.float32
        ),
        ("dp", "red"),
        scatter_dimension=0,
        tiled=True,
    )
    grad_weights = lax.all_gather(owned_rows, "dp", axis=0, tiled=True)
    kernel_total, gain_total = lax.psum((kernel_part, gain_part), ("dp", "red"))
    return (
        module_output,
        frame_gradient,
        grad_weights * grad_scale,
        kernel_total * grad_scale,
        gain_total * grad_scale,
    )


def solution(mesh):
    placed = (
        P(("dp", "red"), None, None),
        P(("dp", "red"), None, None),
        P("red", None),
        P(),
        P(),
        P(),
    )
    return jax.shard_map(
        local,
        mesh=mesh,
        in_specs=placed,
        out_specs=(
            P(("dp", "red"), None, None),
            P(("dp", "red"), None, None),
            P("red", None),
            P(),
            P(),
        ),
        check_vma=False,
    )
```

profile of v0, /device:TPU:0, one launch (start us, length us, event | category | flops | bytes accessed | tf_op | source)
XLA Modules:
  0.0 923.1 jit_solution(477016552205187638)
XLA Ops:
  8.8 2.1 convert_reduce_fusion
  12.2 2.2 fusion.11
  14.4 8.3 copy.13
  22.7 10.6 %reshape_reshape.3 = bf16[768,8,16,12]{0,3,2,1:T(8,128)(2,1)} reshape(bf16[16,48,1536]{1,0,2:T(8,128)(2,1)} %copy.13) | data formatting | bytes 4718592 | tf_op jit(solution)/shard_map/reshape;reshape | solution.py:101
  33.3 4.1 copy.14
  37.4 5.0 reshape.139
  43.6 23.0 %all-gather.4.cloned.1.call-done = bf16[1536,3072]{1,0:T(8,128)(2,1)} async-done(((bf16[192,3072]{1,0:T(8,128)(2,1)}), bf16[1536,3072]{1,0:T(8,128)(2,1)}) %all-gather.4.cloned.1.call-update) | async-done | bytes 9437200 | tf_op jit(solution)/shard_map/all_gather | solution.py:88
  66.6 10.8 %fusion.3 = f32[16,48,3072]{2,1,0:T(8,128)S(1)} fusion(bf16[16,48,1536]{2,1,0:T(8,128)(2,1)} %fusion.11, bf16[1536,3072]{1,0:T(8,128)(2,1)} %all-gather.4.cloned.1.call-done), kind=kOutput, calls=%fused_computation.62 | convolution fusion | flops 7247757312 | bytes 21233664 | tf_op jit(solution)/shard_map/dot_general | solution.py:23
  78.7 2.7 copy-done.3
  81.4 49.2 %multiply_reduce_fusion = (f32[1536]{0:T(1024)}, f32[1536]{0:T(1024)}, f32[1536]{0:T(1024)}, f32[1536]{0:T(1024)}, f32[1536]{0:T(1024)}, /*index=5*/f32[1536]{0:...) fusion(f32[16,48,1536]{2,1,0:T(8,128)S(1)} %multiply_multiply_f, ...), kind=kLoop, calls=%fused_computation.186 | loop fusion | flops 150981120 | bytes 16856064 | tf_op jit(solution)/shard_map/reduce_sum | solution.py:50
  130.8 28.6 %multiply_convert_fusion.1 = (bf16[16,48,1536]{2,1,0:T(8,128)(2,1)S(1)}, f32[16,48,1536]{2,1,0:T(8,128)}) fusion(f32[16,48,3072]{2,1,0:T(8,128)} %copy-done.3, f32[16,48]{1,0:T(8,128)S(1)} %get-tuple-element.106, f32[16,48]{1,0:T(8,128)S(1)} %get-tuple-element.76, f32[1536]{0:T(1024)} %copy-done.57, f32[16,48]{1,0:T(8,128)S(1)} %get-tuple-element.77, ...), kind=kLoop, calls=%fused_computation.218 | loop fusion | flops 114425856 | bytes 16800768 | tf_op jit(solution)/shard_map/convert.4
  159.4 6.9 multiply_convert_fusion
  167.7 10.8 %fusion.119 = f32[1536,3072]{1,0:T(8,128)} fusion(bf16[768,1536]{0,1:T(8,128)(2,1)S(1)} %copy-done.8, bf16[768,1536]{1,0:T(8,128)(2,1)S(1)} %bitcast.24, bf16[768,1536]{1,0:T(8,128)(2,1)S(1)} %bitcast.23), kind=kOutput, calls=%fused_computation.182 | convolution fusion | flops 7257194496 | bytes 25952256 | tf_op jit(solution)/shard_map/dot_general | solution.py:104
  178.6 366.8 %fusion = f32[16,3072]{1,0:T(8,128)S(1)} fusion(f32[1536,3072]{1,0:T(8,128)} %fusion.119), kind=kCustom, calls=%all-reduce-scatter | all-reduce-scatter fusion | flops 6291457 | bytes 19070976
  557.5 2.9 collective-permute-done.28
  561.8 2.9 collective-permute-done.27
  564.7 4.4 collective-permute-start.22
  570.8 5.6 collective-permute-start.21
  576.5 8.8 collective-permute-done.25
  586.5 9.2 %collective-permute-done.24 = f32[16,3072]{1,0:T(8,128)S(1)} collective-permute-done((f32[16,3072]{1,0:T(8,128)S(1)}, f32[16,3072]{1,0:T(8,128)S(1)}, u32[]{:S(2)}, u32[]{:S(2)}) %collective-permute-start.24) | collective-permute-done | bytes 196640
  595.8 2.0 collective-permute-start.19
  597.9 2.0 collective-permute-start.18
  599.9 2.0 collective-permute-start.17
  601.8 2.0 collective-permute-start.16
  603.8 2.0 collective-permute-start.15
  609.0 11.5 %collective-permute-start.13 = (f32[16,3072]{1,0:T(8,128)S(1)}, f32[16,3072]{1,0:T(8,128)S(1)}, u32[]{:S(2)}, u32[]{:S(2)}) collective-permute-start(f32[16,3072]{1,0:T(8,128)S(1)} %fusion), channel_id=1, source_target_pairs={{0,14},{1,15},{2,16},{3,17},{4,18},{5,19},{6,20},{7,21},{8,22},{9,... | collective-permute-start | bytes 589832
  620.5 9.4 %collective-permute-start.12 = (f32[16,3072]{1,0:T(8,128)S(1)}, f32[16,3072]{1,0:T(8,128)S(1)}, u32[]{:S(2)}, u32[]{:S(2)}) collective-permute-start(f32[16,3072]{1,0:T(8,128)S(1)} %fusion), channel_id=1, source_target_pairs={{0,13},{1,14},{2,15},{3,16},{4,17},{5,18},{6,19},{7,20},{8,21},{9,... | collective-permute-start | bytes 589832
  629.9 3.5 collective-permute-start.11
  633.5 6.5 collective-permute-start.10
  640.0 26.0 %multiply_reduce_fusion.9 = (f32[1536]{0:T(1024)S(1)}, f32[1536]{0:T(1024)S(1)}, f32[1536]{0:T(1024)S(1)}, f32[1536]{0:T(1024)S(1)}, f32[1536]{0:T(1024)S(1)}, /...) fusion(f32[16,48,1536]{2,1,0:T(8,128)} %copy-done.1, f32[16,48,1536]{2,1,0:T(8,128)} %copy-done, ...), kind=kLoop, calls=%fused_computation.195 | loop fusion | flops 30657024 | bytes 9517056 | tf_op jit(solution)/shard_map/reduce_sum | solution.py:50
  667.5 11.3 %collective-permute-start.8 = (f32[16,3072]{1,0:T(8,128)S(1)}, f32[16,3072]{1,0:T(8,128)S(1)}, u32[]{:S(2)}, u32[]{:S(2)}) collective-permute-start(f32[16,3072]{1,0:T(8,128)S(1)} %fusion), channel_id=1, source_target_pairs={{0,9},{1,10},{2,11},{3,12},{4,13},{5,14},{6,15},{7,16},{8,17},{9,1... | collective-permute-start | bytes 589832
  680.2 3.5 collective-permute-start.6
  684.4 3.3 collective-permute-start.5
  687.8 9.0 multiply_reduce_fusion.18
  696.9 5.3 collective-permute-start.4
  702.1 3.7 collective-permute-start.3
  705.9 2.0 collective-permute-start.2
  707.8 3.0 collective-permute-start.1
  711.6 3.0 collective-permute-start
  714.6 3.9 multiply_reduce_fusion.27
  719.0 2.7 stack.127
  722.0 84.8 %concatenate.17 = f32[524,3072]{1,0:T(8,128)} concatenate(f32[12,3072]{1,0:T(8,128)S(1)} %collective-permute-done.31, f32[16,3072]{1,0:T(8,128)S(1)} %collective-permute-done.30, f32[16,3072]{1,0:T(8,128)} %copy-done.9, f32[16,3072]{1,0:T(8,128)} %copy-done.10, f32[16,3072]{1,0:T(8,128)} %copy-done.11, f32[16,3072]{1,0:T(8,128)} %copy-done.12, f32[16,3072]{1,0:T(8,128)} %copy-done.13, ...), dimensions={0} | concatenate | bytes 12877824
  808.5 14.3 %fusion.18 = (f32[1536]{0:T(1024)S(1)}, f32[16,48]{1,0:T(8,128)S(1)}, f32[16,48]{1,0:T(8,128)S(1)}, f32[16,48,1536]{2,1,0:T(8,128)}) fusion(bf16[16,48,1536]{2,1,0:T(8,128)(2,1)S(1)} %copy-done.4, f32[16,48]{1,0:T(8,128)S(1)} %copy-done.60, f32[16,48]{1,0:T(8,128)S(1)} %copy-done.52, f32[1536]{0:T(1024)S(1)} %copy-done.62, ...), kind=kOutput, calls=%fused_computation.80 | convolution fusion | flops 7267808256 | bytes 21258240 | tf_op jit(solution)/shard_map/dot_general | solution.py:67
  822.7 63.5 %psum.15 = f32[1536]{0:T(1024)S(1)} all-reduce(f32[1536]{0:T(1024)S(1)} %get-tuple-element.36), channel_id=1, replica_groups=mesh['dp'=16,'red'=8] {'dp','red'}, use_global_device_ids=true, to_apply=%region_39.40 | all-reduce | flops 1536 | bytes 12288 | tf_op jit(solution)/shard_map/psum | solution.py:112
  886.8 7.8 fusion.17
  896.3 13.4 %all-gather.6.cloned.1.call-done = f32[16,12,3072]{2,1,0:T(8,128)} async-done(((f32[1,12,3072]{2,1,0:T(8,128)}), f32[16,12,3072]{2,1,0:T(8,128)}) %all-gather.6.cloned.1.call-update) | async-done | bytes 2359312 | tf_op jit(solution)/shard_map/all_gather | solution.py:111
  909.6 3.9 broadcast_multiply_fusion
  913.5 3.0 reshape.143
  (248 shorter events, 34.1 us)
Async XLA Ops:
  7.2 59.4 %all-gather.4.cloned.1.call-start = ((), (), s32[]{:S(2)}) async-start(), calls=%async_computation | async-start | bytes 10616832 | tf_op jit(solution)/shard_map/all_gather | solution.py:88
  7.9 886.8 %all-reduce.7.cloned.1.call-start = ((), (), s32[]{:S(2)}) async-start(), calls=%async_computation.1 | async-start | bytes 393216 | tf_op jit(solution)/shard_map/psum | solution.py:112
  43.2 87.4 %copy-start.42 = (f32[16,48]{1,0:T(8,128)}, f32[16,48]{1,0:T(8,128)S(1)}, u32[]{:S(2)}) copy-start(f32[16,48]{1,0:T(8,128)S(1)} %get-tuple-element.89) | copy-start | bytes 9220
  43.3 87.4 %copy-start.44 = (f32[16,48]{1,0:T(8,128)}, f32[16,48]{1,0:T(8,128)S(1)}, u32[]{:S(2)}) copy-start(f32[16,48]{1,0:T(8,128)S(1)} %get-tuple-element.90) | copy-start | bytes 9220
  43.3 87.4 %copy-start.45 = (f32[16,48]{1,0:T(8,128)}, f32[16,48]{1,0:T(8,128)S(1)}, u32[]{:S(2)}) copy-start(f32[16,48]{1,0:T(8,128)S(1)} %get-tuple-element.91) | copy-start | bytes 9220
  43.3 87.4 %copy-start.46 = (f32[16,48]{1,0:T(8,128)}, f32[16,48]{1,0:T(8,128)S(1)}, u32[]{:S(2)}) copy-start(f32[16,48]{1,0:T(8,128)S(1)} %get-tuple-element.92) | copy-start | bytes 9220
  43.3 87.4 %copy-start.47 = (f32[16,48]{1,0:T(8,128)}, f32[16,48]{1,0:T(8,128)S(1)}, u32[]{:S(2)}) copy-start(f32[16,48]{1,0:T(8,128)S(1)} %get-tuple-element.93) | copy-start | bytes 9220
  43.4 87.3 %copy-start.48 = (f32[16,48]{1,0:T(8,128)}, f32[16,48]{1,0:T(8,128)S(1)}, u32[]{:S(2)}) copy-start(f32[16,48]{1,0:T(8,128)S(1)} %get-tuple-element.94) | copy-start | bytes 9220
  43.4 87.3 %copy-start.49 = (f32[16,48]{1,0:T(8,128)}, f32[16,48]{1,0:T(8,128)S(1)}, u32[]{:S(2)}) copy-start(f32[16,48]{1,0:T(8,128)S(1)} %get-tuple-element.95) | copy-start | bytes 9220
  43.4 87.3 %copy-start.50 = (f32[16,48]{1,0:T(8,128)}, f32[16,48]{1,0:T(8,128)S(1)}, u32[]{:S(2)}) copy-start(f32[16,48]{1,0:T(8,128)S(1)} %get-tuple-element.96) | copy-start | bytes 9220
  43.5 87.2 %copy-start.30 = (f32[16,48]{1,0:T(8,128)}, f32[16,48]{1,0:T(8,128)S(1)}, u32[]{:S(2)}) copy-start(f32[16,48]{1,0:T(8,128)S(1)} %get-tuple-element.79) | copy-start | bytes 9220
  43.5 87.2 %copy-start.32 = (f32[16,48]{1,0:T(8,128)}, f32[16,48]{1,0:T(8,128)S(1)}, u32[]{:S(2)}) copy-start(f32[16,48]{1,0:T(8,128)S(1)} %get-tuple-element.80) | copy-start | bytes 9220
  43.5 87.2 %copy-start.34 = (f32[16,48]{1,0:T(8,128)}, f32[16,48]{1,0:T(8,128)S(1)}, u32[]{:S(2)}) copy-start(f32[16,48]{1,0:T(8,128)S(1)} %get-tuple-element.81) | copy-start | bytes 9220
  178.6 427.3 %copy-start.72 = (s32[2048]{0:T(1024)S(1)}, s32[2048]{0:T(1024)}, u32[]{:S(2)}) copy-start(s32[2048]{0:T(1024)} %param.11) | copy-start | bytes 24580
  178.6 461.4 %copy-start.43 = (f32[16,48]{1,0:T(8,128)S(1)}, f32[16,48]{1,0:T(8,128)}, u32[]{:S(2)}) copy-start(f32[16,48]{1,0:T(8,128)} %copy-done.42) | copy-start | bytes 9220
  545.4 7.9 collective-permute-start.30
  546.7 5.2 collective-permute-start.31
  548.0 8.2 collective-permute-start.29
  549.3 11.1 %collective-permute-start.28 = (f32[16,3072]{1,0:T(8,128)S(1)}, f32[16,3072]{1,0:T(8,128)S(1)}, u32[]{:S(2)}, u32[]{:S(2)}) collective-permute-start(f32[16,3072]{1,0:T(8,128)S(1)} %fusion), channel_id=1, source_target_pairs={{0,29},{1,30},{2,31},{3,32},{4,33},{5,34},{6,35},{7,36},{8,37},{9,... | collective-permute-start | bytes 589832
  550.7 14.0 %collective-permute-start.27 = (f32[16,3072]{1,0:T(8,128)S(1)}, f32[16,3072]{1,0:T(8,128)S(1)}, u32[]{:S(2)}, u32[]{:S(2)}) collective-permute-start(f32[16,3072]{1,0:T(8,128)S(1)} %fusion), channel_id=1, source_target_pairs={{0,28},{1,29},{2,30},{3,31},{4,32},{5,33},{6,34},{7,35},{8,36},{9,... | collective-permute-start | bytes 589832
  552.0 18.9 %collective-permute-start.26 = (f32[16,3072]{1,0:T(8,128)S(1)}, f32[16,3072]{1,0:T(8,128)S(1)}, u32[]{:S(2)}, u32[]{:S(2)}) collective-permute-start(f32[16,3072]{1,0:T(8,128)S(1)} %fusion), channel_id=1, source_target_pairs={{0,27},{1,28},{2,29},{3,30},{4,31},{5,32},{6,33},{7,34},{8,35},{9,... | collective-permute-start | bytes 589832
  553.3 32.0 %collective-permute-start.25 = (f32[16,3072]{1,0:T(8,128)S(1)}, f32[16,3072]{1,0:T(8,128)S(1)}, u32[]{:S(2)}, u32[]{:S(2)}) collective-permute-start(f32[16,3072]{1,0:T(8,128)S(1)} %fusion), channel_id=1, source_target_pairs={{0,26},{1,27},{2,28},{3,29},{4,30},{5,31},{6,32},{7,33},{8,34},{9,... | collective-permute-start | bytes 589832
  556.2 39.5 %collective-permute-start.24 = (f32[16,3072]{1,0:T(8,128)S(1)}, f32[16,3072]{1,0:T(8,128)S(1)}, u32[]{:S(2)}, u32[]{:S(2)}) collective-permute-start(f32[16,3072]{1,0:T(8,128)S(1)} %fusion), channel_id=1, source_target_pairs={{0,25},{1,26},{2,27},{3,28},{4,29},{5,30},{6,31},{7,32},{8,33},{9,... | collective-permute-start | bytes 589832
  560.5 37.4 %collective-permute-start.23 = (f32[16,3072]{1,0:T(8,128)S(1)}, f32[16,3072]{1,0:T(8,128)S(1)}, u32[]{:S(2)}, u32[]{:S(2)}) collective-permute-start(f32[16,3072]{1,0:T(8,128)S(1)} %fusion), channel_id=1, source_target_pairs={{0,24},{1,25},{2,26},{3,27},{4,28},{5,29},{6,30},{7,31},{8,32},{9,... | collective-permute-start | bytes 589832
  564.7 35.2 %collective-permute-start.22 = (f32[16,3072]{1,0:T(8,128)S(1)}, f32[16,3072]{1,0:T(8,128)S(1)}, u32[]{:S(2)}, u32[]{:S(2)}) collective-permute-start(f32[16,3072]{1,0:T(8,128)S(1)} %fusion), channel_id=1, source_target_pairs={{0,23},{1,24},{2,25},{3,26},{4,27},{5,28},{6,29},{7,30},{8,31},{9,... | collective-permute-start | bytes 589832
  570.8 31.0 %collective-permute-start.21 = (f32[16,3072]{1,0:T(8,128)S(1)}, f32[16,3072]{1,0:T(8,128)S(1)}, u32[]{:S(2)}, u32[]{:S(2)}) collective-permute-start(f32[16,3072]{1,0:T(8,128)S(1)} %fusion), channel_id=1, source_target_pairs={{0,22},{1,23},{2,24},{3,25},{4,26},{5,27},{6,28},{7,29},{8,30},{9,... | collective-permute-start | bytes 589832
  585.3 18.6 %collective-permute-start.20 = (f32[16,3072]{1,0:T(8,128)S(1)}, f32[16,3072]{1,0:T(8,128)S(1)}, u32[]{:S(2)}, u32[]{:S(2)}) collective-permute-start(f32[16,3072]{1,0:T(8,128)S(1)} %fusion), channel_id=1, source_target_pairs={{0,21},{1,22},{2,23},{3,24},{4,25},{5,26},{6,27},{7,28},{8,29},{9,... | collective-permute-start | bytes 589832
  595.8 11.6 %collective-permute-start.19 = (f32[16,3072]{1,0:T(8,128)S(1)}, f32[16,3072]{1,0:T(8,128)}, u32[]{:S(2)}, u32[]{:S(2)}) collective-permute-start(f32[16,3072]{1,0:T(8,128)S(1)} %fusion), channel_id=1, source_target_pairs={{0,20},{1,21},{2,22},{3,23},{4,24},{5,25},{6,26},{7,27},{8,28},{9,... | collective-permute-start | bytes 589832
  597.9 11.1 %collective-permute-start.18 = (f32[16,3072]{1,0:T(8,128)S(1)}, f32[16,3072]{1,0:T(8,128)}, u32[]{:S(2)}, u32[]{:S(2)}) collective-permute-start(f32[16,3072]{1,0:T(8,128)S(1)} %fusion), channel_id=1, source_target_pairs={{0,19},{1,20},{2,21},{3,22},{4,23},{5,24},{6,25},{7,26},{8,27},{9,... | collective-permute-start | bytes 589832
  599.9 20.6 %collective-permute-start.17 = (f32[16,3072]{1,0:T(8,128)S(1)}, f32[16,3072]{1,0:T(8,128)}, u32[]{:S(2)}, u32[]{:S(2)}) collective-permute-start(f32[16,3072]{1,0:T(8,128)S(1)} %fusion), channel_id=1, source_target_pairs={{0,18},{1,19},{2,20},{3,21},{4,22},{5,23},{6,24},{7,25},{8,26},{9,... | collective-permute-start | bytes 589832
  601.8 28.1 %collective-permute-start.16 = (f32[16,3072]{1,0:T(8,128)S(1)}, f32[16,3072]{1,0:T(8,128)}, u32[]{:S(2)}, u32[]{:S(2)}) collective-permute-start(f32[16,3072]{1,0:T(8,128)S(1)} %fusion), channel_id=1, source_target_pairs={{0,17},{1,18},{2,19},{3,20},{4,21},{5,22},{6,23},{7,24},{8,25},{9,... | collective-permute-start | bytes 589832
  603.8 29.6 %collective-permute-start.15 = (f32[16,3072]{1,0:T(8,128)S(1)}, f32[16,3072]{1,0:T(8,128)}, u32[]{:S(2)}, u32[]{:S(2)}) collective-permute-start(f32[16,3072]{1,0:T(8,128)S(1)} %fusion), channel_id=1, source_target_pairs={{0,16},{1,17},{2,18},{3,19},{4,20},{5,21},{6,22},{7,23},{8,24},{9,... | collective-permute-start | bytes 589832
  607.4 58.5 %collective-permute-start.14 = (f32[16,3072]{1,0:T(8,128)S(1)}, f32[16,3072]{1,0:T(8,128)S(1)}, u32[]{:S(2)}, u32[]{:S(2)}) collective-permute-start(f32[16,3072]{1,0:T(8,128)S(1)} %fusion), channel_id=1, source_target_pairs={{0,15},{1,16},{2,17},{3,18},{4,19},{5,20},{6,21},{7,22},{8,23},{9,... | collective-permute-start | bytes 589832
  609.0 58.5 %collective-permute-start.13 = (f32[16,3072]{1,0:T(8,128)S(1)}, f32[16,3072]{1,0:T(8,128)S(1)}, u32[]{:S(2)}, u32[]{:S(2)}) collective-permute-start(f32[16,3072]{1,0:T(8,128)S(1)} %fusion), channel_id=1, source_target_pairs={{0,14},{1,15},{2,16},{3,17},{4,18},{5,19},{6,20},{7,21},{8,22},{9,... | collective-permute-start | bytes 589832
  620.5 58.3 %collective-permute-start.12 = (f32[16,3072]{1,0:T(8,128)S(1)}, f32[16,3072]{1,0:T(8,128)S(1)}, u32[]{:S(2)}, u32[]{:S(2)}) collective-permute-start(f32[16,3072]{1,0:T(8,128)S(1)} %fusion), channel_id=1, source_target_pairs={{0,13},{1,14},{2,15},{3,16},{4,17},{5,18},{6,19},{7,20},{8,21},{9,... | collective-permute-start | bytes 589832
  629.9 50.2 %collective-permute-start.11 = (f32[16,3072]{1,0:T(8,128)S(1)}, f32[16,3072]{1,0:T(8,128)S(1)}, u32[]{:S(2)}, u32[]{:S(2)}) collective-permute-start(f32[16,3072]{1,0:T(8,128)S(1)} %fusion), channel_id=1, source_target_pairs={{0,12},{1,13},{2,14},{3,15},{4,16},{5,17},{6,18},{7,19},{8,20},{9,... | collective-permute-start | bytes 589832
  633.5 50.2 %collective-permute-start.10 = (f32[16,3072]{1,0:T(8,128)S(1)}, f32[16,3072]{1,0:T(8,128)S(1)}, u32[]{:S(2)}, u32[]{:S(2)}) collective-permute-start(f32[16,3072]{1,0:T(8,128)S(1)} %fusion), channel_id=1, source_target_pairs={{0,11},{1,12},{2,13},{3,14},{4,15},{5,16},{6,17},{7,18},{8,19},{9,... | collective-permute-start | bytes 589832
  666.0 30.9 %collective-permute-start.9 = (f32[16,3072]{1,0:T(8,128)S(1)}, f32[16,3072]{1,0:T(8,128)S(1)}, u32[]{:S(2)}, u32[]{:S(2)}) collective-permute-start(f32[16,3072]{1,0:T(8,128)S(1)} %fusion), channel_id=1, source_target_pairs={{0,10},{1,11},{2,12},{3,13},{4,14},{5,15},{6,16},{7,17},{8,18},{9,... | collective-permute-start | bytes 589832
  667.5 34.6 %collective-permute-start.8 = (f32[16,3072]{1,0:T(8,128)S(1)}, f32[16,3072]{1,0:T(8,128)S(1)}, u32[]{:S(2)}, u32[]{:S(2)}) collective-permute-start(f32[16,3072]{1,0:T(8,128)S(1)} %fusion), channel_id=1, source_target_pairs={{0,9},{1,10},{2,11},{3,12},{4,13},{5,14},{6,15},{7,16},{8,17},{9,1... | collective-permute-start | bytes 589832
  678.8 27.0 %collective-permute-start.7 = (f32[16,3072]{1,0:T(8,128)S(1)}, f32[16,3072]{1,0:T(8,128)S(1)}, u32[]{:S(2)}, u32[]{:S(2)}) collective-permute-start(f32[16,3072]{1,0:T(8,128)S(1)} %fusion), channel_id=1, source_target_pairs={{0,8},{1,9},{2,10},{3,11},{4,12},{5,13},{6,14},{7,15},{8,16},{9,17... | collective-permute-start | bytes 589832
  680.2 27.7 %collective-permute-start.6 = (f32[16,3072]{1,0:T(8,128)S(1)}, f32[16,3072]{1,0:T(8,128)S(1)}, u32[]{:S(2)}, u32[]{:S(2)}) collective-permute-start(f32[16,3072]{1,0:T(8,128)S(1)} %fusion), channel_id=1, source_target_pairs={{0,7},{1,8},{2,9},{3,10},{4,11},{5,12},{6,13},{7,14},{8,15},{9,16}... | collective-permute-start | bytes 589832
  684.4 26.5 %collective-permute-start.5 = (f32[16,3072]{1,0:T(8,128)S(1)}, f32[16,3072]{1,0:T(8,128)S(1)}, u32[]{:S(2)}, u32[]{:S(2)}) collective-permute-start(f32[16,3072]{1,0:T(8,128)S(1)} %fusion), channel_id=1, source_target_pairs={{0,6},{1,7},{2,8},{3,9},{4,10},{5,11},{6,12},{7,13},{8,14},{9,15},... | collective-permute-start | bytes 589832
  696.9 25.0 %collective-permute-start.4 = (f32[16,3072]{1,0:T(8,128)S(1)}, f32[16,3072]{1,0:T(8,128)}, u32[]{:S(2)}, u32[]{:S(2)}) collective-permute-start(f32[16,3072]{1,0:T(8,128)S(1)} %fusion), channel_id=1, source_target_pairs={{0,5},{1,6},{2,7},{3,8},{4,9},{5,10},{6,11},{7,12},{8,13},{9,14},{... | collective-permute-start | bytes 589832
  702.1 19.8 %collective-permute-start.3 = (f32[16,3072]{1,0:T(8,128)S(1)}, f32[16,3072]{1,0:T(8,128)}, u32[]{:S(2)}, u32[]{:S(2)}) collective-permute-start(f32[16,3072]{1,0:T(8,128)S(1)} %fusion), channel_id=1, source_target_pairs={{0,4},{1,5},{2,6},{3,7},{4,8},{5,9},{6,10},{7,11},{8,12},{9,13},{1... | collective-permute-start | bytes 589832
  705.9 16.1 %collective-permute-start.2 = (f32[16,3072]{1,0:T(8,128)S(1)}, f32[16,3072]{1,0:T(8,128)}, u32[]{:S(2)}, u32[]{:S(2)}) collective-permute-start(f32[16,3072]{1,0:T(8,128)S(1)} %fusion), channel_id=1, source_target_pairs={{0,3},{1,4},{2,5},{3,6},{4,7},{5,8},{6,9},{7,10},{8,11},{9,12},{10... | collective-permute-start | bytes 589832
  707.8 14.1 %collective-permute-start.1 = (f32[16,3072]{1,0:T(8,128)S(1)}, f32[16,3072]{1,0:T(8,128)}, u32[]{:S(2)}, u32[]{:S(2)}) collective-permute-start(f32[16,3072]{1,0:T(8,128)S(1)} %fusion), channel_id=1, source_target_pairs={{0,2},{1,3},{2,4},{3,5},{4,6},{5,7},{6,8},{7,9},{8,10},{9,11},{10,... | collective-permute-start | bytes 589832
  711.6 10.3 %collective-permute-start = (f32[16,3072]{1,0:T(8,128)S(1)}, f32[16,3072]{1,0:T(8,128)}, u32[]{:S(2)}, u32[]{:S(2)}) collective-permute-start(f32[16,3072]{1,0:T(8,128)S(1)} %fusion), channel_id=1, source_target_pairs={{0,1},{1,2},{2,3},{3,4},{4,5},{5,6},{6,7},{7,8},{8,9},{9,10},{10,1... | collective-permute-start | bytes 589832
  721.9 187.8 %all-gather.6.cloned.1.call-start = ((), (), s32[]{:S(2)}) async-start(), calls=%async_computation.2 | async-start | bytes 3342336 | tf_op jit(solution)/shard_map/all_gather | solution.py:111
  (62 other events, 2057.7 us)
Sparse Core Ops, SparseCore 0:
  9.7 56.8 all-gather.3
  721.9 139.3 all-reduce.6
  863.7 45.8 all-gather.5
where the time goes:
time: 927 us; the launch traced here: 923 us
  blocking collectives  430 us (46%)
  other arithmetic  145 us (16%)
  local copies, waits for them, and re-layouts  128 us (14%)
  starting transfers between devices  103 us (11%)
  waiting for transfers between devices  64.5 us (7%)
  matrix products  35.9 us (4%)
  between operations  16.1 us (2%)
    unnamed x1, blocking collectives  367 us
    unnamed x32, starting transfers between devices  103 us
    unnamed x153, local copies, waits for them, and re-layouts  92.8 us
    reduce_sum x4, other arithmetic, block_pass(): kernel_terms.append(jnp.sum(grad_conv * window * same_seg, axis=(0, 1)))  88.1 us
    psum x1, blocking collectives, local(): kernel_total, gain_total = lax.psum((kernel_part, gain_part), ('dp', 'red'))  63.5 us
    another operation x2, other arithmetic  35.5 us
    unnamed x35, waiting for transfers between devices  28.2 us
    all_gather x1, waiting for transfers between devices, local(): weights = lax.all_gather(w_in, 'red', axis=0, tiled=True)  23 us
  transfers between devices with their start and end apart: 35, of which 9 were waited for; matrix products, arithmetic and copies ran while one was open for 20% of the time, Pallas kernels for 0%

commit v1 on v0

v1 whole, which is shorter than its diff:
```python
import functools

import jax
import jax.numpy as jnp
from jax import lax
from jax.experimental import pallas as pl
from jax.experimental.pallas import tpu as pltpu
from jax.sharding import PartitionSpec as P

EPSILON = 1e-05
D = 1536
K = 31
R = K // 2
U = 16
L = 48
N = U * L
C = 256
C2 = 2 * C
NB = D // C
LT = C // 128
T = 8
RB = 192
RX = RB // 4
MESH = pl.DeviceIdType.MESH
f32 = jnp.float32
bf16 = jnp.bfloat16


def sigmoid(x):
    return 0.5 * jnp.tanh(0.5 * x) + 0.5


def aligned(i, n):
    return pl.ds(pl.multiple_of(i, n), n)


def body(
    frames, cot, w, kern, gain, lens,
    mo_o, fg_o, gw_o, gk_o, gg_o,
    nat0, nat1, pm, pmt, fr, up, mean, istd, sc, sct, W, gh, h, glu, gcp, mot, kg, len16, gs,
    own, sibs, sibr, s1s, s1r, s2s, s2r, gwp,
    kgl, kgsr, kg1, kg1r, kg2, kg2r, kgo, ggl, ggr, gg2, gg2r, gg3, gg3r,
    in_sem, mo_sem, wl_sem, wz_s, wz_r, ws_s, ws_r,
    ss_s, ss_r, s1_s, s1_r, s2_s, s2_r, s3_s, s3_r, s3_l,
    ks_s, ks_r, k1_s, k1_r, k2_s, k2_r, k3_s, k3_r, g_s, g_r,
):
    dp, red = lax.axis_index("dp"), lax.axis_index("red")
    x, y = lax.div(dp, 4), lax.rem(dp, 4)
    z, c = lax.div(red, 2), lax.rem(red, 2)

    def turn(a, d):
        return lax.rem(a + d, 4)

    def at(ax, ay, az, ac):
        return (ax * 4 + ay, az * 2 + ac)

    sib = at(x, y, z, 1 - c)

    def remote(src, dst, ssem, rsem, dev):
        return pltpu.make_async_remote_copy(
            src_ref=src, dst_ref=dst, send_sem=ssem, recv_sem=rsem, device_id=dev, device_id_type=MESH
        )

    def first(b, d):
        p = lax.rem(b, 2)
        return at(turn(x, d * (1 - p)), turn(y, d * p), z, c)

    def plane(b, d, dz):
        p = lax.rem(b, 2)
        return at(turn(x, d * p), turn(y, d * (1 - p)), turn(z, dz), c)

    def place(b):
        p = lax.rem(b, 2)
        return x * (1 - p) + y * p, x * p + y * (1 - p)

    in0 = pltpu.make_async_copy(frames, nat0, in_sem.at[0])
    in0.start()

    def own_w(b, half):
        return pltpu.make_async_copy(
            w.at[:, aligned(half * D + b * C, C)], W.at[b, red, :, pl.ds(half * C, C)], wl_sem.at[b, half]
        )

    for b in range(NB):
        own_w(b, 0).start()
        own_w(b, 1).start()
    in1 = pltpu.make_async_copy(cot, nat1, in_sem.at[1])
    in1.start()

    barrier = pltpu.get_barrier_semaphore()
    offsets = [
        (i, j, k) for i in range(4) for j in range(4) for k in range(4) if (i, j, k) != (0, 0, 0) and i * j * k == 0
    ]
    pl.semaphore_signal(barrier, inc=1, device_id=sib, device_id_type=MESH)
    for i, j, k in offsets:
        pl.semaphore_signal(barrier, inc=1, device_id=at(turn(x, i), turn(y, j), turn(z, k), c), device_id_type=MESH)
    pl.semaphore_wait(barrier, len(offsets) + 1)

    def wz(b, j):
        return remote(W.at[b, red], W.at[b, red], wz_s.at[b, j - 1], wz_r.at[b, j - 1], at(x, y, turn(z, j), c))

    def wsib(b, j):
        held = turn(z, 4 - j) * 2 + c
        return remote(W.at[b, held], W.at[b, held], ws_s.at[b, j], ws_r.at[b, j], sib)

    def send_w(b, _):
        own_w(b, 0).wait()
        own_w(b, 1).wait()
        for j in (1, 3, 2):
            wz(b, j).start()
        wsib(b, 0).start()
        return 0

    def forward_w(b):
        for j in (1, 3, 2):
            wz(b, j).wait_recv()
            wsib(b, j).start()

    def arrived_w(b):
        for j in range(4):
            wsib(b, j).wait_recv()

    def sent_w(b, _):
        for j in (1, 2, 3):
            wz(b, j).wait_send()
        for j in range(4):
            wsib(b, j).wait_send()
        return 0

    lax.fori_loop(0, NB, send_w, 0)

    r0 = lax.broadcasted_iota(jnp.int32, (N, N), 0)
    r1 = lax.broadcasted_iota(jnp.int32, (N, N), 1)
    pm[...] = jnp.where(((r0 & 15) * L + (r0 >> 4)) == r1, 1.0, 0.0).astype(bf16)
    pmt[...] = jnp.where(((r1 & 15) * L + (r1 >> 4)) == r0, 1.0, 0.0).astype(bf16)
    me = dp * 8 + red
    row = lens[pl.ds(lax.div(me, 8), 1), :]
    sub = lax.broadcasted_iota(jnp.int32, (U, 128), 0)
    lane = lax.broadcasted_iota(jnp.int32, (U, 128), 1)
    mine = jnp.where(lane == sub + lax.rem(me, 8) * U, row, 0)
    len16[...] = jnp.broadcast_to(jnp.sum(mine, axis=1, keepdims=True), (U, 128))
    every = jnp.sum(jnp.sum(lens[...], axis=0, keepdims=True), axis=1, keepdims=True)
    root = lax.rsqrt(every.astype(f32))
    glu[...] = jnp.zeros_like(glu)
    gcp[...] = jnp.zeros_like(gcp)
    gg3[...] = jnp.zeros_like(gg3)

    def live(t0, n, lanes):
        t = lax.broadcasted_iota(jnp.int32, (n, U, lanes), 0) + t0
        return t < len16[:, :lanes][None]

    in0.wait()
    PR = 256

    def perm_frames(i, _):
        rows = aligned(i * PR, PR)
        fr[rows, :] = jnp.dot(pm[rows, :], nat0[...], preferred_element_type=f32).astype(bf16)
        return 0

    lax.fori_loop(0, N // PR, perm_frames, 0)

    def norm(i, _):
        NR = 128
        rows = aligned(i * NR, NR)
        v = fr[rows, :].astype(f32)
        m = jnp.mean(v, axis=-1, keepdims=True)
        cen = v - m
        s = lax.rsqrt(jnp.mean(cen * cen, axis=-1, keepdims=True) + EPSILON)
        mean[rows, :] = m
        istd[rows, :] = s
        scaled = cen * s * gain[...]
        sc[rows, :] = scaled.astype(bf16)
        turned = scaled.T.astype(bf16)
        for q in range(8):
            other = lax.rem(c + q % 2, 2)
            dst = other * (4 * RB) + (q // 2) * RB
            sct[aligned_rows(dst, RB), rows] = turned[q * RB : (q + 1) * RB, :]
        return 0

    def aligned_rows(i, n):
        return pl.ds(pl.multiple_of(i, 64), n)

    lax.fori_loop(0, N // 128, norm, 0)
    in1.wait()

    def perm_cot(i, _):
        rows = aligned(i * PR, PR)
        v = jnp.dot(pm[rows, :], nat1[...], preferred_element_type=f32).reshape(PR // U, U, D)
        up[rows, :] = jnp.where(live(i * (PR // U), PR // U, 1), v, 0.0).reshape(PR, D).astype(bf16)
        return 0

    lax.fori_loop(0, N // PR, perm_cot, 0)

    def sib_send(b):
        return remote(sibs.at[lax.rem(b, 2)], sibr.at[b], ss_s.at[lax.rem(b, 2)], ss_r.at[b], sib)

    def ksib(b):
        return remote(kgl.at[b], kgsr.at[b], ks_s.at[b], ks_r.at[b], sib)

    def s1(b, j):
        p = lax.rem(b, 2)
        f, _ = place(b)
        return remote(s1s.at[p, turn(f, j)], s1r.at[b, j - 1], s1_s.at[p, j - 1], s1_r.at[b, j - 1], first(b, j))

    def k1(b, j):
        f, _ = place(b)
        return remote(kg1.at[b, turn(f, j)], kg1r.at[b, j - 1], k1_s.at[b, j - 1], k1_r.at[b, j - 1], first(b, j))

    def s2(b, i):
        p = lax.rem(b, 2)
        _, s = place(b)
        d, dz = lax.div(i, 4), lax.rem(i, 4)
        return remote(
            s2s.at[p, turn(s, d), turn(z, dz)], s2r.at[b, i - 1], s2_s.at[p, i - 1], s2_r.at[b, i - 1], plane(b, d, dz)
        )

    def k2(b, i):
        d, dz = lax.div(i, 4), lax.rem(i, 4)
        return remote(kg2.at[b], kg2r.at[b, i - 1], k2_s.at[b, i - 1], k2_r.at[b, i - 1], plane(b, d, dz))

    def piece(b):
        f, s = place(b)
        return gw_o.at[aligned(f * RX, RX), aligned(lax.div(s, 2) * D + b * C + lax.rem(s, 2) * 128, 128)]

    def s3(b, i):
        dev = at(turn(x, lax.div(i, 4)), turn(y, lax.rem(i, 4)), z, c)
        return remote(gwp.at[b], piece(b), s3_s.at[b, i - 1], s3_r.at[b, i - 1], dev)

    def s3_own(b):
        return pltpu.make_async_copy(gwp.at[b], piece(b), s3_l.at[b])

    def k3(b, j):
        f, _ = place(b)
        return remote(kgo.at[b, f], kgo.at[b, f], k3_s.at[b, j - 1], k3_r.at[b, j - 1], first(b, j))

    def loop15(fn):
        def step(i, _):
            fn(i)
            return 0

        lax.fori_loop(1, 16, step, 0)

    def stage1(b):
        p = lax.rem(b, 2)
        sib_send(b).wait_recv()

        @pl.when(b >= 2)
        def _():
            for j in (1, 2, 3):
                s1(b - 2, j).wait_send()

        def add(q, _):
            v = own[q] + sibr[b, q].astype(f32)
            for f in range(4):
                s1s[p, f, q] = v[f * RX : (f + 1) * RX].astype(bf16)
            return 0

        lax.fori_loop(0, 4, add, 0)
        for j in (1, 3, 2):
            s1(b, j).start()
        ksib(b).wait_recv()
        t = kgl[b] + kgsr[b]
        for f in range(4):
            kg1[b, f] = t[f * 8 : (f + 1) * 8]
        for j in (1, 3, 2):
            k1(b, j).start()

    def stage2(b):
        p = lax.rem(b, 2)
        f, _ = place(b)
        for j in (1, 2, 3):
            s1(b, j).wait_recv()

        @pl.when(b >= 2)
        def _():
            loop15(lambda i: s2(b - 2, i).wait_send())

        def add(q, _):
            v = s1s[p, f, q].astype(f32)
            for j in range(3):
                v = v + s1r[b, j, q].astype(f32)
            for s in range(4):
                s2s[p, s, q] = v[:, s * 128 : (s + 1) * 128].astype(bf16)
            return 0

        lax.fori_loop(0, 4, add, 0)
        loop15(lambda i: s2(b, i).start())
        for j in (1, 2, 3):
            k1(b, j).wait_recv()
        kg2[b] = kg1[b, f] + kg1r[b, 0] + kg1r[b, 1] + kg1r[b, 2]
        loop15(lambda i: k2(b, i).start())

    def stage3(b):
        p = lax.rem(b, 2)
        f, s = place(b)
        loop15(lambda i: s2(b, i).wait_recv())
        v = s2s[p, s, z].astype(f32)
        for i in range(15):
            v = v + s2r[b, i].astype(f32)
        gwp[b] = (v * root).astype(bf16)
        loop15(lambda i: s3(b, i).start())
        s3_own(b).start()
        loop15(lambda i: k2(b, i).wait_recv())
        t = kg2[b]
        for i in range(15):
            t = t + kg2r[b, i]
        kgo[b, f] = t * root
        for j in (1, 2, 3):
            k3(b, j).start()

    def block(b, _):
        forward_first = b == 0

        @pl.when(forward_first)
        def _():
            forward_w(b)

        arrived_w(b)

        def hidden(i, _):
            rows = aligned(i * 256, 256)
            h[rows, :] = jnp.dot(sc[rows, :], W[b].reshape(D, C2), preferred_element_type=f32)
            return 0

        lax.fori_loop(0, N // 256, hidden, 0)

        @pl.when(b >= 1)
        def _():
            stage1(b - 1)

        for lt in range(LT):
            vl = slice(lt * 128, (lt + 1) * 128)
            gl = slice(C + lt * 128, C + (lt + 1) * 128)
            cl = aligned(b * C + lt * 128, 128)

            def gate(i, _):
                rows = aligned(i * (T * U), T * U)
                s = sigmoid(h[rows, gl])
                h[rows, gl] = s
                out = jnp.where(live(i * T, T, 128), (h[rows, vl] * s).reshape(T, U, 128), 0.0)
                glu[lt, pl.ds(i * T + R, T)] = out
                return 0

            lax.fori_loop(0, L // T, gate, 0)
            kg[...] = jnp.zeros_like(kg)

            def forward(i, _):
                t0 = i * T
                rows = aligned(i * (T * U), T * U)
                acc = jnp.zeros((T, U, 128), f32)
                for k in range(K):
                    acc = acc + kern[k : k + 1, cl][None] * glu[lt, pl.ds(t0 + k, T)]
                s = sigmoid(acc)
                swish = acc * s
                out = jnp.where(live(t0, T, 128), fr[rows, cl].astype(f32).reshape(T, U, 128) + swish, 0.0)
                mot[rows, vl] = out.reshape(T * U, 128).astype(bf16)
                gc = up[rows, cl].astype(f32).reshape(T, U, 128) * (s + swish * (1.0 - s))
                gcp[lt, pl.ds(t0 + R, T)] = gc
                for k in range(K):
                    p = jnp.sum(gc * glu[lt, pl.ds(t0 + k, T)], axis=0)
                    kg[k] += p[0:8] + p[8:16]
                return 0

            lax.fori_loop(0, L // T, forward, 0)
            kgl[b, :, vl] = jnp.sum(kg[...], axis=1)

            def backward(i, _):
                t0 = i * T
                rows = aligned(i * (T * U), T * U)
                acc = jnp.zeros((T, U, 128), f32)
                for k in range(K):
                    acc = acc + kern[k : k + 1, cl][None] * gcp[lt, pl.ds(t0 + (K - 1) - k, T)]
                dg = jnp.where(live(t0, T, 128), acc, 0.0)
                s = h[rows, gl].reshape(T, U, 128)
                gh[b, rows, vl] = (dg * s).reshape(T * U, 128).astype(bf16)
                gate_part = dg * glu[lt, pl.ds(t0 + R, T)] * (1.0 - s)
                gh[b, rows, gl] = gate_part.reshape(T * U, 128).astype(bf16)
                return 0

            lax.fori_loop(0, L // T, backward, 0)

        @pl.when(b + 1 < NB)
        def _():
            forward_w(b + 1)

        @pl.when(b >= 2)
        def _():
            sib_send(b - 2).wait_send()

        def dw_other(i, _):
            rows = aligned(i * 2 * RB + 4 * RB, 2 * RB)
            g = jnp.dot(sct[rows, :], gh[b], preferred_element_type=f32).astype(bf16)
            sibs[lax.rem(b, 2), pl.ds(2 * i, 2)] = g.reshape(2, RB, C2)
            return 0

        lax.fori_loop(0, 2, dw_other, 0)
        sib_send(b).start()
        ksib(b).start()

        def dw_own(i, _):
            rows = aligned(i * 2 * RB, 2 * RB)
            g = jnp.dot(sct[rows, :], gh[b], preferred_element_type=f32)
            own[pl.ds(2 * i, 2)] = g.reshape(2, RB, C2)
            return 0

        lax.fori_loop(0, 2, dw_own, 0)

        @pl.when(b >= 3)
        def _():
            stage3(b - 3)

        @pl.when(b >= 2)
        def _():
            stage2(b - 2)

        cols = aligned(b * C, C)

        def perm_out(i, _):
            rows = aligned(i * PR, PR)
            nat0[rows, cols] = jnp.dot(pmt[rows, :], mot[...], preferred_element_type=f32).astype(bf16)
            return 0

        lax.fori_loop(0, N // PR, perm_out, 0)
        mo_copy(b).start()
        return 0

    def mo_copy(b):
        cols = aligned(b * C, C)
        return pltpu.make_async_copy(nat0.at[:, cols], mo_o.at[:, cols], mo_sem.at[b])

    lax.fori_loop(0, NB, block, 0)

    stage3(NB - 3)
    stage2(NB - 2)
    stage1(NB - 1)
    ggl[...] = jnp.zeros_like(ggl)
    FR = 256

    def final(i, _):
        rows = aligned(i * FR, FR)

        def acc(b, _):
            p = lax.dot_general(
                gh[b, rows, :], W[b].reshape(D, C2), (((1,), (1,)), ((), ())), preferred_element_type=f32
            )

            @pl.when(b == 0)
            def _():
                gs[...] = p

            @pl.when(b > 0)
            def _():
                gs[...] += p

            return 0

        lax.fori_loop(0, NB, acc, 0)

        @pl.when(i == 1)
        def _():
            stage3(NB - 2)

        @pl.when(i == 2)
        def _():
            stage2(NB - 1)

        def ln(j, _):
            NR = 64
            part = aligned(j * NR, NR)
            r = pl.ds(pl.multiple_of(i * FR + j * NR, NR), NR)
            g0 = gs[part, :]
            s = istd[r, :]
            nm = (fr[r, :].astype(f32) - mean[r, :]) * s
            ggl[...] += jnp.sum((g0 * nm).reshape(NR // 8, 8, D), axis=0)
            g = g0 * gain[...]
            m1 = jnp.mean(g, axis=-1, keepdims=True)
            m2 = jnp.mean(g * nm, axis=-1, keepdims=True)
            o = up[r, :].astype(f32) + s * (g - m1 - nm * m2)
            lv = live(i * (FR // U) + j * (NR // U), NR // U, 1)
            nat1[r, :] = jnp.where(lv, o.reshape(NR // U, U, D), 0.0).reshape(NR, D).astype(bf16)
            return 0

        lax.fori_loop(0, FR // 64, ln, 0)
        return 0

    lax.fori_loop(0, N // FR, final, 0)

    total = jnp.sum(ggl[...], axis=0, keepdims=True)
    for q in range(D // 128):
        gg3[q : q + 1, :] = total[:, q * 128 : (q + 1) * 128]

    def g1():
        return remote(gg3, ggr, g_s.at[18], g_r.at[18], sib)

    def g2(i):
        return remote(gg2, gg2r.at[i - 1], g_s.at[i - 1], g_r.at[i - 1], plane(0, lax.div(i, 4), lax.rem(i, 4)))

    def g3(j):
        return remote(ggl2, gg3r.at[j - 1], g_s.at[14 + j], g_r.at[14 + j], first(0, j))

    ggl2 = ggl.at[:, 0:256]
    g1().start()

    def mo_done(b, _):
        mo_copy(b).wait()
        return 0

    lax.fori_loop(0, NB, mo_done, 0)

    def perm_grad(i, _):
        rows = aligned(i * PR, PR)
        nat0[rows, :] = jnp.dot(pmt[rows, :], nat1[...], preferred_element_type=f32).astype(bf16)
        return 0

    g1().wait_recv()
    gg2[...] = gg3[...] + ggr[...]
    loop15(lambda i: g2(i).start())
    stage3(NB - 1)
    lax.fori_loop(0, N // PR, perm_grad, 0)
    fg_copy = pltpu.make_async_copy(nat0, fg_o, in_sem.at[0])
    fg_copy.start()
    loop15(lambda i: g2(i).wait_recv())
    t = gg2[...]
    for i in range(15):
        t = t + gg2r[i]
    ggl[:, 0:128] = t[0:8]
    ggl[:, 128:256] = t[8:16]
    for j in (1, 2, 3):
        g3(j).start()

    def done(b, _):
        loop15(lambda i: s3(b, i).wait())
        s3_own(b).wait()
        for j in (1, 2, 3):
            k3(b, j).wait()
            k1(b, j).wait_send()
        ksib(b).wait_send()
        loop15(lambda i: k2(b, i).wait_send())
        gk_o[:, aligned(b * C, C)] = kgo[b].reshape(32, C)[0:K]
        return 0

    lax.fori_loop(0, NB, done, 0)
    lax.fori_loop(0, NB, sent_w, 0)
    for b in (NB - 2, NB - 1):
        sib_send(b).wait_send()
        for j in (1, 2, 3):
            s1(b, j).wait_send()
        loop15(lambda i: s2(b, i).wait_send())
    g1().wait_send()
    loop15(lambda i: g2(i).wait_send())
    for j in (1, 2, 3):
        g3(j).wait()
    t = (ggl[:, 0:256] + gg3r[0] + gg3r[1] + gg3r[2]) * root
    for q in range(D // 128):
        gg_o[0:1, q * 128 : (q + 1) * 128] = t[q % 8 : q % 8 + 1, (q // 8) * 128 : (q // 8 + 1) * 128]
    fg_copy.wait()


def local(frames, cotangent, w_in, kernel, gain, lengths):
    V, DMA = pltpu.VMEM, pltpu.SemaphoreType.DMA
    far = pl.BlockSpec(memory_space=pl.ANY)
    near = pl.BlockSpec(memory_space=pltpu.VMEM)
    mo, fg, gw, gk, gg = pl.pallas_call(
        body,
        out_shape=[
            jax.ShapeDtypeStruct((N, D), bf16),
            jax.ShapeDtypeStruct((N, D), bf16),
            jax.ShapeDtypeStruct((RB, 2 * D), bf16),
            jax.ShapeDtypeStruct((K, D), f32),
            jax.ShapeDtypeStruct((1, D), f32),
        ],
        in_specs=[far, far, far, near, near, near],
        out_specs=[far, far, far, near, near],
        scratch_shapes=[
            V((N, D), bf16), V((N, D), bf16), V((N, N), bf16), V((N, N), bf16), V((N, D), bf16), V((N, D), bf16),
            V((N, 1), f32), V((N, 1), f32), V((N, D), bf16), V((D, N), bf16),
            V((NB, 8, RB, C2), bf16), V((NB, N, C2), bf16), V((N, C2), f32),
            V((LT, L + 2 * R, U, 128), f32), V((LT, L + 2 * R, U, 128), f32), V((N, C), bf16),
            V((K + 1, 8, 128), f32), V((U, 128), jnp.int32), V((256, D), f32),
            V((4, RB, C2), f32), V((2, 4, RB, C2), bf16), V((NB, 4, RB, C2), bf16),
            V((2, 4, 4, RX, C2), bf16), V((NB, 3, 4, RX, C2), bf16),
            V((2, 4, 4, RX, 128), bf16), V((NB, 15, RX, 128), bf16), V((NB, RX, 128), bf16),
            V((NB, 32, C), f32), V((NB, 32, C), f32), V((NB, 4, 8, C), f32), V((NB, 3, 8, C), f32),
            V((NB, 8, C), f32), V((NB, 15, 8, C), f32), V((NB, 4, 8, C), f32),
            V((8, D), f32), V((16, 128), f32), V((16, 128), f32), V((15, 16, 128), f32),
            V((16, 128), f32), V((3, 8, 256), f32),
            DMA((2,)), DMA((NB,)), DMA((NB, 2)), DMA((NB, 3)), DMA((NB, 3)), DMA((NB, 4)), DMA((NB, 4)),
            DMA((2,)), DMA((NB,)), DMA((2, 3)), DMA((NB, 3)), DMA((2, 15)), DMA((NB, 15)),
            DMA((NB, 15)), DMA((NB, 15)), DMA((NB,)),
            DMA((NB,)), DMA((NB,)), DMA((NB, 3)), DMA((NB, 3)), DMA((NB, 15)), DMA((NB, 15)),
            DMA((NB, 3)), DMA((NB, 3)), DMA((19,)), DMA((19,)),
        ],
        compiler_params=pltpu.CompilerParams(collective_id=0, has_side_effects=True, vmem_limit_bytes=62 << 20),
    )(
        frames.reshape(N, D),
        cotangent.reshape(N, D),
        w_in,
        kernel,
        gain.reshape(1, D),
        lengths.reshape(16, 128),
    )
    return mo.reshape(U, L, D), fg.reshape(U, L, D), gw.astype(f32), gk, gg.reshape(D)


def solution(mesh):
    rows = P(("dp", "red"), None, None)
    return jax.shard_map(
        local,
        mesh=mesh,
        in_specs=(rows, rows, P("red", None), P(), P(), P()),
        out_specs=(rows, rows, P("red", None), P(), P()),
        check_vma=False,
    )
```

time: 927 us -> 153 us (0.17)
  blocking collectives: 430 us -> 0 us
  Pallas kernels: 0 us -> 142 us
  other arithmetic: 145 us -> 3.7 us
  local copies, waits for them, and re-layouts: 128 us -> 5.91 us
  starting transfers between devices: 103 us -> 0 us
  waiting for transfers between devices: 64.5 us -> 0 us
  matrix products: 35.9 us -> 0 us
  between operations: 16.1 us -> 0.66 us
    unnamed x1 -> x0, blocking collectives: 367 us -> none
    pallas_call x0 -> x1, Pallas kernels: none -> 142 us  [local(): pl.pallas_call(body, out_shape=[jax.ShapeDtypeStruct((N, D), bf16), jax.S...]
    unnamed x32 -> x0, starting transfers between devices: 103 us -> none
    reduce_sum x7 -> x0, other arithmetic: 91.6 us -> none  [the longest x4 88.1 us: block_pass(): kernel_terms.append(jnp.sum(grad_conv * window * same_seg, axis=(0, 1)))]
    unnamed x153 -> x11, local copies, waits for them, and re-layouts: 92.8 us -> 4.61 us
    psum x1 -> x0, blocking collectives: 63.5 us -> none  [local(): kernel_total, gain_total = lax.psum((kernel_part, gain_part), ('dp', 'red'))]
    all_gather x2 -> x0, waiting for transfers between devices: 36.3 us -> none  [the longest x1 23 us: local(): weights = lax.all_gather(w_in, 'red', axis=0, tiled=True)]
    dot_general x3 -> x0, matrix products: 35.9 us -> none  [the longest x1 14.3 us: block_pass(): lax.dot_general(flat_grad, weights, (((1,), (1,)), ((), ())), preferred_e...]
  transfers between devices with their start and end apart: 35 -> 0, of which waited for: 9 -> 0; matrix products, arithmetic and copies ran while one was open for 20% -> 0% of each run, Pallas kernels for 0% -> 0%
where the time goes in v1:
time: 153 us
  Pallas kernels  142 us (93%)
  local copies, waits for them, and re-layouts  5.91 us (4%)
  other arithmetic  3.7 us (2%)
    pallas_call x1, Pallas kernels, local(): pl.pallas_call(body, out_shape=[jax.ShapeDtypeStruct((N, D), bf16), jax.S...  142 us
    unnamed x11, local copies, waits for them, and re-layouts  4.61 us
    convert_element_type x1, other arithmetic, local(): gw.astype(f32)  3.09 us

profile of v1, /device:TPU:0, one launch (start us, length us, event | category | flops | bytes accessed | tf_op | source)
XLA Modules:
  0.0 152.5 jit_solution(7497506713783652967)
XLA Ops:
  0.6 1.3 reshape.33.gain
  1.9 142.3 %shard_map.101 = (bf16[768,1536]{1,0:T(8,128)(2,1)}, bf16[768,1536]{1,0:T(8,128)(2,1)}, bf16[192,3072]{1,0:T(8,128)(2,1)}, f32[31,1536]{1,0:T(8,128)}, f32[1,1536]{1,0:T(1,128)}) custom-call(bf16[768,1536]{1,0:T(8,128)(2,1)} %bitcast.5, bf16[768,1536]{1,0:T(8,128)(2,1)} %bitcast.6, bf16[192,3072]{1,0:T(8,128)(2,1)} %w.1, f32[31,1536]{1,0:T(8,128)} %kern.1, ...), custom_call_target="tpu_custom_call" | custom-call | tf_op jit(solution)/shard_map/pallas_call | solution.py:563
  144.2 0.0 copy-start.3
  144.2 0.0 copy-start.1
  144.2 3.1 %convert_element_type.3 = f32[192,3072]{1,0:T(8,128)} convert(bf16[192,3072]{1,0:T(8,128)(2,1)} %get-tuple-element.12) | non-fusion elementwise | flops 589824 | bytes 3538944 | tf_op jit(solution)/shard_map/convert_element_type | solution.py:602
  147.3 0.0 copy-done.3
  147.3 0.6 reduce
  147.9 0.0 copy-done.1
  147.9 0.0 copy-start
  147.9 1.4 copy.14
  149.3 1.1 copy-done
  150.4 0.0 copy-start.2
  150.4 1.4 copy.15
  151.8 0.0 copy-done.2
  151.9 0.7 copy.16
Async XLA Ops:
  144.2 3.1 %copy-start.3 = (f32[1,1536]{1,0:T(1,128)S(1)}, f32[1,1536]{1,0:T(1,128)}, u32[]{:S(2)}) copy-start(f32[1,1536]{1,0:T(1,128)} %get-tuple-element.14) | copy-start | bytes 18436
  144.2 3.7 %copy-start.1 = (bf16[768,1536]{1,0:T(8,128)(2,1)S(1)}, bf16[768,1536]{1,0:T(8,128)(2,1)}, u32[]{:S(2)}) copy-start(bf16[768,1536]{1,0:T(8,128)(2,1)} %get-tuple-element.10) | copy-start | bytes 7077892
  147.9 2.5 %copy-start = (bf16[768,1536]{1,0:T(8,128)(2,1)S(1)}, bf16[768,1536]{1,0:T(8,128)(2,1)}, u32[]{:S(2)}) copy-start(bf16[768,1536]{1,0:T(8,128)(2,1)} %get-tuple-element.11) | copy-start | bytes 7077892
  150.4 1.4 copy-start.2

commit v2 on v1

--- a/solution.py
+++ b/solution.py
@@ -39,7 +39,7 @@
     mo_o, fg_o, gw_o, gk_o, gg_o,
     nat0, nat1, pm, pmt, fr, up, mean, istd, sc, sct, W, gh, h, glu, gcp, mot, kg, len16, gs,
     own, sibs, sibr, s1s, s1r, s2s, s2r, gwp,
-    kgl, kgsr, kg1, kg1r, kg2, kg2r, kgo, ggl, ggr, gg2, gg2r, gg3, gg3r,
+    kgl, kgsr, kg1, kg1r, kg2, kg2r, kgo, ggl, ggr, gg2, gg2r, gg3, gg3r, gg4,
     in_sem, mo_sem, wl_sem, wz_s, wz_r, ws_s, ws_r,
     ss_s, ss_r, s1_s, s1_r, s2_s, s2_r, s3_s, s3_r, s3_l,
     ks_s, ks_r, k1_s, k1_r, k2_s, k2_r, k3_s, k3_r, g_s, g_r,
@@ -159,6 +159,8 @@
 
     lax.fori_loop(0, N // PR, perm_frames, 0)
 
+    gain_row = jnp.concatenate([gain[q : q + 1, :] for q in range(D // 128)], axis=1)
+
     def norm(i, _):
         NR = 128
         rows = aligned(i * NR, NR)
@@ -168,7 +170,7 @@
         s = lax.rsqrt(jnp.mean(cen * cen, axis=-1, keepdims=True) + EPSILON)
         mean[rows, :] = m
         istd[rows, :] = s
-        scaled = cen * s * gain[...]
+        scaled = cen * s * gain_row
         sc[rows, :] = scaled.astype(bf16)
         turned = scaled.T.astype(bf16)
         for q in range(8):
@@ -317,12 +319,7 @@
 
         arrived_w(b)
 
-        def hidden(i, _):
-            rows = aligned(i * 256, 256)
-            h[rows, :] = jnp.dot(sc[rows, :], W[b].reshape(D, C2), preferred_element_type=f32)
-            return 0
-
-        lax.fori_loop(0, N // 256, hidden, 0)
+        h[...] = jnp.dot(sc[...], W[b].reshape(D, C2), preferred_element_type=f32)
 
         @pl.when(b >= 1)
         def _():
@@ -387,23 +384,12 @@
         def _():
             sib_send(b - 2).wait_send()
 
-        def dw_other(i, _):
-            rows = aligned(i * 2 * RB + 4 * RB, 2 * RB)
-            g = jnp.dot(sct[rows, :], gh[b], preferred_element_type=f32).astype(bf16)
-            sibs[lax.rem(b, 2), pl.ds(2 * i, 2)] = g.reshape(2, RB, C2)
-            return 0
-
-        lax.fori_loop(0, 2, dw_other, 0)
+        g = jnp.dot(sct[4 * RB :, :], gh[b], preferred_element_type=f32).astype(bf16)
+        sibs[lax.rem(b, 2)] = g.reshape(4, RB, C2)
         sib_send(b).start()
         ksib(b).start()
 
-        def dw_own(i, _):
-            rows = aligned(i * 2 * RB, 2 * RB)
-            g = jnp.dot(sct[rows, :], gh[b], preferred_element_type=f32)
-            own[pl.ds(2 * i, 2)] = g.reshape(2, RB, C2)
-            return 0
-
-        lax.fori_loop(0, 2, dw_own, 0)
+        own[...] = jnp.dot(sct[: 4 * RB, :], gh[b], preferred_element_type=f32).reshape(4, RB, C2)
 
         @pl.when(b >= 3)
         def _():
@@ -415,12 +401,7 @@
 
         cols = aligned(b * C, C)
 
-        def perm_out(i, _):
-            rows = aligned(i * PR, PR)
-            nat0[rows, cols] = jnp.dot(pmt[rows, :], mot[...], preferred_element_type=f32).astype(bf16)
-            return 0
-
-        lax.fori_loop(0, N // PR, perm_out, 0)
+        nat0[:, cols] = jnp.dot(pmt[...], mot[...], preferred_element_type=f32).astype(bf16)
         mo_copy(b).start()
         return 0
 
@@ -434,99 +415,90 @@
     stage2(NB - 2)
     stage1(NB - 1)
     ggl[...] = jnp.zeros_like(ggl)
-    FR = 256
-
-    def final(i, _):
-        rows = aligned(i * FR, FR)
-
-        def acc(b, _):
-            p = lax.dot_general(
-                gh[b, rows, :], W[b].reshape(D, C2), (((1,), (1,)), ((), ())), preferred_element_type=f32
-            )
-
-            @pl.when(b == 0)
-            def _():
-                gs[...] = p
-
-            @pl.when(b > 0)
-            def _():
-                gs[...] += p
-
-            return 0
-
-        lax.fori_loop(0, NB, acc, 0)
-
-        @pl.when(i == 1)
+
+    def g1():
+        return remote(gg3, ggr, g_s.at[18], g_r.at[18], sib)
+
+    def g2(i):
+        return remote(gg2, gg2r.at[i - 1], g_s.at[i - 1], g_r.at[i - 1], plane(0, lax.div(i, 4), lax.rem(i, 4)))
+
+    def g3(j):
+        return remote(gg4, gg3r.at[j - 1], g_s.at[14 + j], g_r.at[14 + j], first(0, j))
+
+    def acc(b, _):
+        p = lax.dot_general(gh[b], W[b].reshape(D, C2), (((1,), (1,)), ((), ())), preferred_element_type=f32)
+
+        @pl.when(b == 0)
+        def _():
+            gs[...] = p
+
+        @pl.when(b > 0)
+        def _():
+            gs[...] += p
+
+        @pl.when(b == 4)
         def _():
             stage3(NB - 2)
 
-        @pl.when(i == 2)
-        def _():
-            stage2(NB - 1)
-
-        def ln(j, _):
-            NR = 64
-            part = aligned(j * NR, NR)
-            r = pl.ds(pl.multiple_of(i * FR + j * NR, NR), NR)
-            g0 = gs[part, :]
-            s = istd[r, :]
-            nm = (fr[r, :].astype(f32) - mean[r, :]) * s
-            ggl[...] += jnp.sum((g0 * nm).reshape(NR // 8, 8, D), axis=0)
-            g = g0 * gain[...]
-            m1 = jnp.mean(g, axis=-1, keepdims=True)
-            m2 = jnp.mean(g * nm, axis=-1, keepdims=True)
-            o = up[r, :].astype(f32) + s * (g - m1 - nm * m2)
-            lv = live(i * (FR // U) + j * (NR // U), NR // U, 1)
-            nat1[r, :] = jnp.where(lv, o.reshape(NR // U, U, D), 0.0).reshape(NR, D).astype(bf16)
-            return 0
-
-        lax.fori_loop(0, FR // 64, ln, 0)
-        return 0
-
-    lax.fori_loop(0, N // FR, final, 0)
-
+        return 0
+
+    lax.fori_loop(0, NB, acc, 0)
+    NR = 64
+
+    def normed(r):
+        return (fr[r, :].astype(f32) - mean[r, :]) * istd[r, :]
+
+    def gain_part(j, _):
+        r = aligned(j * NR, NR)
+        ggl[...] += jnp.sum((gs[r, :] * normed(r)).reshape(NR // 8, 8, D), axis=0)
+        return 0
+
+    lax.fori_loop(0, N // NR, gain_part, 0)
     total = jnp.sum(ggl[...], axis=0, keepdims=True)
     for q in range(D // 128):
         gg3[q : q + 1, :] = total[:, q * 128 : (q + 1) * 128]
-
-    def g1():
-        return remote(gg3, ggr, g_s.at[18], g_r.at[18], sib)
-
-    def g2(i):
-        return remote(gg2, gg2r.at[i - 1], g_s.at[i - 1], g_r.at[i - 1], plane(0, lax.div(i, 4), lax.rem(i, 4)))
-
-    def g3(j):
-        return remote(ggl2, gg3r.at[j - 1], g_s.at[14 + j], g_r.at[14 + j], first(0, j))
-
-    ggl2 = ggl.at[:, 0:256]
     g1().start()
+
+    def ln(j, _):
+        @pl.when(j == 3)
+        def _():
+            g1().wait_recv()
+            gg2[...] = gg3[...] + ggr[...]
+            loop15(lambda i: g2(i).start())
+
+        @pl.when(j == 7)
+        def _():
+            stage2(NB - 1)
+
+        r = aligned(j * NR, NR)
+        s = istd[r, :]
+        nm = normed(r)
+        g = gs[r, :] * gain_row
+        m1 = jnp.mean(g, axis=-1, keepdims=True)
+        m2 = jnp.mean(g * nm, axis=-1, keepdims=True)
+        o = up[r, :].astype(f32) + s * (g - m1 - nm * m2)
+        lv = live(j * (NR // U), NR // U, 1)
+        nat1[r, :] = jnp.where(lv, o.reshape(NR // U, U, D), 0.0).reshape(NR, D).astype(bf16)
+        return 0
+
+    lax.fori_loop(0, N // NR, ln, 0)
 
     def mo_done(b, _):
         mo_copy(b).wait()
         return 0
 
     lax.fori_loop(0, NB, mo_done, 0)
-
-    def perm_grad(i, _):
-        rows = aligned(i * PR, PR)
-        nat0[rows, :] = jnp.dot(pmt[rows, :], nat1[...], preferred_element_type=f32).astype(bf16)
-        return 0
-
-    g1().wait_recv()
-    gg2[...] = gg3[...] + ggr[...]
-    loop15(lambda i: g2(i).start())
-    stage3(NB - 1)
-    lax.fori_loop(0, N // PR, perm_grad, 0)
+    nat0[...] = jnp.dot(pmt[...], nat1[...], preferred_element_type=f32).astype(bf16)
     fg_copy = pltpu.make_async_copy(nat0, fg_o, in_sem.at[0])
     fg_copy.start()
     loop15(lambda i: g2(i).wait_recv())
     t = gg2[...]
     for i in range(15):
         t = t + gg2r[i]
-    ggl[:, 0:128] = t[0:8]
-    ggl[:, 128:256] = t[8:16]
+    gg4[...] = t
     for j in (1, 2, 3):
         g3(j).start()
+    stage3(NB - 1)
 
     def done(b, _):
         loop15(lambda i: s3(b, i).wait())
@@ -550,9 +522,7 @@
     loop15(lambda i: g2(i).wait_send())
     for j in (1, 2, 3):
         g3(j).wait()
-    t = (ggl[:, 0:256] + gg3r[0] + gg3r[1] + gg3r[2]) * root
-    for q in range(D // 128):
-        gg_o[0:1, q * 128 : (q + 1) * 128] = t[q % 8 : q % 8 + 1, (q // 8) * 128 : (q // 8 + 1) * 128]
+    gg_o[...] = ((gg4[...] + gg3r[0] + gg3r[1] + gg3r[2]) * root)[0 : D // 128]
     fg_copy.wait()
 
 
@@ -567,7 +537,7 @@
             jax.ShapeDtypeStruct((N, D), bf16),
             jax.ShapeDtypeStruct((RB, 2 * D), bf16),
             jax.ShapeDtypeStruct((K, D), f32),
-            jax.ShapeDtypeStruct((1, D), f32),
+            jax.ShapeDtypeStruct((D // 128, 128), f32),
         ],
         in_specs=[far, far, far, near, near, near],
         out_specs=[far, far, far, near, near],
@@ -576,14 +546,14 @@
             V((N, 1), f32), V((N, 1), f32), V((N, D), bf16), V((D, N), bf16),
             V((NB, 8, RB, C2), bf16), V((NB, N, C2), bf16), V((N, C2), f32),
             V((LT, L + 2 * R, U, 128), f32), V((LT, L + 2 * R, U, 128), f32), V((N, C), bf16),
-            V((K + 1, 8, 128), f32), V((U, 128), jnp.int32), V((256, D), f32),
+            V((K + 1, 8, 128), f32), V((U, 128), jnp.int32), V((N, D), f32),
             V((4, RB, C2), f32), V((2, 4, RB, C2), bf16), V((NB, 4, RB, C2), bf16),
             V((2, 4, 4, RX, C2), bf16), V((NB, 3, 4, RX, C2), bf16),
             V((2, 4, 4, RX, 128), bf16), V((NB, 15, RX, 128), bf16), V((NB, RX, 128), bf16),
             V((NB, 32, C), f32), V((NB, 32, C), f32), V((NB, 4, 8, C), f32), V((NB, 3, 8, C), f32),
             V((NB, 8, C), f32), V((NB, 15, 8, C), f32), V((NB, 4, 8, C), f32),
             V((8, D), f32), V((16, 128), f32), V((16, 128), f32), V((15, 16, 128), f32),
-            V((16, 128), f32), V((3, 8, 256), f32),
+            V((16, 128), f32), V((3, 16, 128), f32), V((16, 128), f32),
             DMA((2,)), DMA((NB,)), DMA((NB, 2)), DMA((NB, 3)), DMA((NB, 3)), DMA((NB, 4)), DMA((NB, 4)),
             DMA((2,)), DMA((NB,)), DMA((2, 3)), DMA((NB, 3)), DMA((2, 15)), DMA((NB, 15)),
             DMA((NB, 15)), DMA((NB, 15)), DMA((NB,)),
@@ -596,7 +566,7 @@
         cotangent.reshape(N, D),
         w_in,
         kernel,
-        gain.reshape(1, D),
+        gain.reshape(D // 128, 128),
         lengths.reshape(16, 128),
     )
     return mo.reshape(U, L, D), fg.reshape(U, L, D), gw.astype(f32), gk, gg.reshape(D)

time: 153 us -> 149 us (0.974)
  Pallas kernels: 142 us -> 140 us
    pallas_call x1, Pallas kernels: 142 us -> 140 us  [local(): pl.pallas_call(body, out_shape=[jax.ShapeDtypeStruct((N, D), bf16), jax.S...]
    unnamed x11 -> x12, local copies, waits for them, and re-layouts: 4.61 us -> 5.21 us
where the time goes in v2:
time: 149 us
  Pallas kernels  140 us (94%)
  local copies, waits for them, and re-layouts  5.21 us (3%)
  other arithmetic  3.09 us (2%)
    pallas_call x1, Pallas kernels, local(): pl.pallas_call(body, out_shape=[jax.ShapeDtypeStruct((N, D), bf16), jax.S...  140 us
    unnamed x12, local copies, waits for them, and re-layouts  5.21 us
    convert_element_type x1, other arithmetic, local(): gw.astype(f32)  3.09 us

profile of v2, /device:TPU:0, one launch (start us, length us, event | category | flops | bytes accessed | tf_op | source)
XLA Modules:
  0.0 148.5 jit_solution(2440617729582870747)
XLA Ops:
  0.6 139.6 %shard_map.101 = (bf16[768,1536]{1,0:T(8,128)(2,1)}, bf16[768,1536]{1,0:T(8,128)(2,1)}, bf16[192,3072]{1,0:T(8,128)(2,1)}, f32[31,1536]{1,0:T(8,128)}, f32[12,128]{1,0:T(8,128)}) custom-call(bf16[768,1536]{1,0:T(8,128)(2,1)} %bitcast.9, bf16[768,1536]{1,0:T(8,128)(2,1)} %bitcast.10, bf16[192,3072]{1,0:T(8,128)(2,1)} %w.1, f32[31,1536]{1,0:T(8,128)} %kern.1, ...), custom_call_target="tpu_custom_call" | custom-call | tf_op jit(solution)/shard_map/pallas_call | solution.py:533
  140.2 0.0 copy-start.1
  140.2 3.1 %convert_element_type.3 = f32[192,3072]{1,0:T(8,128)} convert(bf16[192,3072]{1,0:T(8,128)(2,1)} %get-tuple-element.12) | non-fusion elementwise | flops 589824 | bytes 3538944 | tf_op jit(solution)/shard_map/convert_element_type | solution.py:572
  143.3 0.0 copy-done.1
  143.3 0.0 copy-start
  143.3 1.4 copy.15
  144.7 1.1 copy-done
  145.8 0.0 copy-start.2
  145.8 0.0 copy-start.3
  145.8 1.4 copy.16
  147.3 0.0 copy-done.2
  147.3 0.7 copy.17
  147.9 0.0 copy-done.3
  147.9 0.6 copy.18
Async XLA Ops:
  140.2 3.1 %copy-start.1 = (bf16[768,1536]{1,0:T(8,128)(2,1)S(1)}, bf16[768,1536]{1,0:T(8,128)(2,1)}, u32[]{:S(2)}) copy-start(bf16[768,1536]{1,0:T(8,128)(2,1)} %get-tuple-element.10) | copy-start | bytes 7077892
  143.3 2.5 %copy-start = (bf16[768,1536]{1,0:T(8,128)(2,1)S(1)}, bf16[768,1536]{1,0:T(8,128)(2,1)}, u32[]{:S(2)}) copy-start(bf16[768,1536]{1,0:T(8,128)(2,1)} %get-tuple-element.11) | copy-start | bytes 7077892
  145.8 1.4 copy-start.2
  145.8 2.1 %copy-start.3 = (f32[12,128]{1,0:T(8,128)S(1)}, f32[12,128]{1,0:T(8,128)}, u32[]{:S(2)}) copy-start(f32[12,128]{1,0:T(8,128)} %get-tuple-element.14) | copy-start | bytes 18436

commit v3 on v2

--- a/solution.py
+++ b/solution.py
@@ -49,7 +49,7 @@
     z, c = lax.div(red, 2), lax.rem(red, 2)
 
     def turn(a, d):
-        return lax.rem(a + d, 4)
+        return (a + d) & 3
 
     def at(ax, ay, az, ac):
         return (ax * 4 + ay, az * 2 + ac)
@@ -197,7 +197,7 @@
         return remote(sibs.at[lax.rem(b, 2)], sibr.at[b], ss_s.at[lax.rem(b, 2)], ss_r.at[b], sib)
 
     def ksib(b):
-        return remote(kgl.at[b], kgsr.at[b], ks_s.at[b], ks_r.at[b], sib)
+        return remote(kgl.at[lax.div(b, 3)], kgsr.at[lax.div(b, 3)], ks_s.at[lax.div(b, 3)], ks_r.at[lax.div(b, 3)], sib)
 
     def s1(b, j):
         p = lax.rem(b, 2)
@@ -206,26 +206,28 @@
 
     def k1(b, j):
         f, _ = place(b)
-        return remote(kg1.at[b, turn(f, j)], kg1r.at[b, j - 1], k1_s.at[b, j - 1], k1_r.at[b, j - 1], first(b, j))
+        g = lax.div(b, 3)
+        return remote(kg1.at[g, turn(f, j)], kg1r.at[g, j - 1], k1_s.at[g, j - 1], k1_r.at[g, j - 1], first(b, j))
 
     def s2(b, i):
         p = lax.rem(b, 2)
         _, s = place(b)
-        d, dz = lax.div(i, 4), lax.rem(i, 4)
+        d, dz = i // 4, i % 4
         return remote(
             s2s.at[p, turn(s, d), turn(z, dz)], s2r.at[b, i - 1], s2_s.at[p, i - 1], s2_r.at[b, i - 1], plane(b, d, dz)
         )
 
     def k2(b, i):
-        d, dz = lax.div(i, 4), lax.rem(i, 4)
-        return remote(kg2.at[b], kg2r.at[b, i - 1], k2_s.at[b, i - 1], k2_r.at[b, i - 1], plane(b, d, dz))
+        d, dz = i // 4, i % 4
+        g = lax.div(b, 3)
+        return remote(kg2.at[g], kg2r.at[g, i - 1], k2_s.at[g, i - 1], k2_r.at[g, i - 1], plane(b, d, dz))
 
     def piece(b):
         f, s = place(b)
         return gw_o.at[aligned(f * RX, RX), aligned(lax.div(s, 2) * D + b * C + lax.rem(s, 2) * 128, 128)]
 
     def s3(b, i):
-        dev = at(turn(x, lax.div(i, 4)), turn(y, lax.rem(i, 4)), z, c)
+        dev = at(turn(x, i // 4), turn(y, i % 4), z, c)
         return remote(gwp.at[b], piece(b), s3_s.at[b, i - 1], s3_r.at[b, i - 1], dev)
 
     def s3_own(b):
@@ -233,14 +235,12 @@
 
     def k3(b, j):
         f, _ = place(b)
-        return remote(kgo.at[b, f], kgo.at[b, f], k3_s.at[b, j - 1], k3_r.at[b, j - 1], first(b, j))
+        g = lax.div(b, 3)
+        return remote(kgo.at[g, f], kgo.at[g, f], k3_s.at[g, j - 1], k3_r.at[g, j - 1], first(b, j))
 
     def loop15(fn):
-        def step(i, _):
+        for i in range(1, 16):
             fn(i)
-            return 0
-
-        lax.fori_loop(1, 16, step, 0)
 
     def stage1(b):
         p = lax.rem(b, 2)
@@ -260,12 +260,16 @@
         lax.fori_loop(0, 4, add, 0)
         for j in (1, 3, 2):
             s1(b, j).start()
-        ksib(b).wait_recv()
-        t = kgl[b] + kgsr[b]
-        for f in range(4):
-            kg1[b, f] = t[f * 8 : (f + 1) * 8]
-        for j in (1, 3, 2):
-            k1(b, j).start()
+
+        @pl.when(lax.rem(b, 3) == 2)
+        def _():
+            g = lax.div(b, 3)
+            ksib(b).wait_recv()
+            t = kgl[g] + kgsr[g]
+            for f in range(4):
+                kg1[g, f] = t[f * 8 : (f + 1) * 8]
+            for j in (1, 3, 2):
+                k1(b, j).start()
 
     def stage2(b):
         p = lax.rem(b, 2)
@@ -287,10 +291,14 @@
 
         lax.fori_loop(0, 4, add, 0)
         loop15(lambda i: s2(b, i).start())
-        for j in (1, 2, 3):
-            k1(b, j).wait_recv()
-        kg2[b] = kg1[b, f] + kg1r[b, 0] + kg1r[b, 1] + kg1r[b, 2]
-        loop15(lambda i: k2(b, i).start())
+
+        @pl.when(lax.rem(b, 3) == 2)
+        def _():
+            g = lax.div(b, 3)
+            for j in (1, 2, 3):
+                k1(b, j).wait_recv()
+            kg2[g] = kg1[g, f] + kg1r[g, 0] + kg1r[g, 1] + kg1r[g, 2]
+            loop15(lambda i: k2(b, i).start())
 
     def stage3(b):
         p = lax.rem(b, 2)
@@ -302,13 +310,30 @@
         gwp[b] = (v * root).astype(bf16)
         loop15(lambda i: s3(b, i).start())
         s3_own(b).start()
-        loop15(lambda i: k2(b, i).wait_recv())
-        t = kg2[b]
-        for i in range(15):
-            t = t + kg2r[b, i]
-        kgo[b, f] = t * root
-        for j in (1, 2, 3):
-            k3(b, j).start()
+
+        @pl.when(lax.rem(b, 3) == 2)
+        def _():
+            g = lax.div(b, 3)
+            loop15(lambda i: k2(b, i).wait_recv())
+            t = kg2[g]
+            for i in range(15):
+                t = t + kg2r[g, i]
+            kgo[g, f] = t * root
+            for j in (1, 2, 3):
+                k3(b, j).start()
+
+    def put_taps(b, lt):
+        kgl[lax.div(b, 3), :, aligned(lax.rem(b, 3) * C + lt * 128, 128)] = jnp.sum(kg[...], axis=1)
+
+    def trimmed(step, at_start, at_end):
+        step(0, at_start)
+
+        def inner(i, _):
+            step(i, range(K))
+            return 0
+
+        lax.fori_loop(1, L // T - 1, inner, 0)
+        step(L // T - 1, at_end)
 
     def block(b, _):
         forward_first = b == 0
@@ -341,11 +366,11 @@
             lax.fori_loop(0, L // T, gate, 0)
             kg[...] = jnp.zeros_like(kg)
 
-            def forward(i, _):
+            def forward(i, taps):
                 t0 = i * T
                 rows = aligned(i * (T * U), T * U)
                 acc = jnp.zeros((T, U, 128), f32)
-                for k in range(K):
+                for k in taps:
                     acc = acc + kern[k : k + 1, cl][None] * glu[lt, pl.ds(t0 + k, T)]
                 s = sigmoid(acc)
                 swish = acc * s
@@ -353,28 +378,26 @@
                 mot[rows, vl] = out.reshape(T * U, 128).astype(bf16)
                 gc = up[rows, cl].astype(f32).reshape(T, U, 128) * (s + swish * (1.0 - s))
                 gcp[lt, pl.ds(t0 + R, T)] = gc
-                for k in range(K):
+                for k in taps:
                     p = jnp.sum(gc * glu[lt, pl.ds(t0 + k, T)], axis=0)
                     kg[k] += p[0:8] + p[8:16]
-                return 0
-
-            lax.fori_loop(0, L // T, forward, 0)
-            kgl[b, :, vl] = jnp.sum(kg[...], axis=1)
-
-            def backward(i, _):
+
+            trimmed(forward, range(T, K), range(K - T))
+            put_taps(b, lt)
+
+            def backward(i, taps):
                 t0 = i * T
                 rows = aligned(i * (T * U), T * U)
                 acc = jnp.zeros((T, U, 128), f32)
-                for k in range(K):
+                for k in taps:
                     acc = acc + kern[k : k + 1, cl][None] * gcp[lt, pl.ds(t0 + (K - 1) - k, T)]
                 dg = jnp.where(live(t0, T, 128), acc, 0.0)
                 s = h[rows, gl].reshape(T, U, 128)
                 gh[b, rows, vl] = (dg * s).reshape(T * U, 128).astype(bf16)
                 gate_part = dg * glu[lt, pl.ds(t0 + R, T)] * (1.0 - s)
                 gh[b, rows, gl] = gate_part.reshape(T * U, 128).astype(bf16)
-                return 0
-
-            lax.fori_loop(0, L // T, backward, 0)
+
+            trimmed(backward, range(K - T), range(T, K))
 
         @pl.when(b + 1 < NB)
         def _():
@@ -387,7 +410,10 @@
         g = jnp.dot(sct[4 * RB :, :], gh[b], preferred_element_type=f32).astype(bf16)
         sibs[lax.rem(b, 2)] = g.reshape(4, RB, C2)
         sib_send(b).start()
-        ksib(b).start()
+
+        @pl.when(lax.rem(b, 3) == 2)
+        def _():
+            ksib(b).start()
 
         own[...] = jnp.dot(sct[: 4 * RB, :], gh[b], preferred_element_type=f32).reshape(4, RB, C2)
 
@@ -411,16 +437,15 @@
 
     lax.fori_loop(0, NB, block, 0)
 
-    stage3(NB - 3)
+    stage1(NB - 1)
     stage2(NB - 2)
-    stage1(NB - 1)
     ggl[...] = jnp.zeros_like(ggl)
 
     def g1():
         return remote(gg3, ggr, g_s.at[18], g_r.at[18], sib)
 
     def g2(i):
-        return remote(gg2, gg2r.at[i - 1], g_s.at[i - 1], g_r.at[i - 1], plane(0, lax.div(i, 4), lax.rem(i, 4)))
+        return remote(gg2, gg2r.at[i - 1], g_s.at[i - 1], g_r.at[i - 1], plane(0, i // 4, i % 4))
 
     def g3(j):
         return remote(gg4, gg3r.at[j - 1], g_s.at[14 + j], g_r.at[14 + j], first(0, j))
@@ -435,6 +460,10 @@
         @pl.when(b > 0)
         def _():
             gs[...] += p
+
+        @pl.when(b == 1)
+        def _():
+            stage3(NB - 3)
 
         @pl.when(b == 4)
         def _():
@@ -466,7 +495,7 @@
             gg2[...] = gg3[...] + ggr[...]
             loop15(lambda i: g2(i).start())
 
-        @pl.when(j == 7)
+        @pl.when(j == 5)
         def _():
             stage2(NB - 1)
 
@@ -503,13 +532,16 @@
     def done(b, _):
         loop15(lambda i: s3(b, i).wait())
         s3_own(b).wait()
+        return 0
+
+    for b in (2, 5):
         for j in (1, 2, 3):
             k3(b, j).wait()
             k1(b, j).wait_send()
         ksib(b).wait_send()
         loop15(lambda i: k2(b, i).wait_send())
-        gk_o[:, aligned(b * C, C)] = kgo[b].reshape(32, C)[0:K]
-        return 0
+        g = b // 3
+        gk_o[:, g * 3 * C : (g + 1) * 3 * C] = kgo[g].reshape(32, 3 * C)[0:K]
 
     lax.fori_loop(0, NB, done, 0)
     lax.fori_loop(0, NB, sent_w, 0)
@@ -550,15 +582,15 @@
             V((4, RB, C2), f32), V((2, 4, RB, C2), bf16), V((NB, 4, RB, C2), bf16),
             V((2, 4, 4, RX, C2), bf16), V((NB, 3, 4, RX, C2), bf16),
             V((2, 4, 4, RX, 128), bf16), V((NB, 15, RX, 128), bf16), V((NB, RX, 128), bf16),
-            V((NB, 32, C), f32), V((NB, 32, C), f32), V((NB, 4, 8, C), f32), V((NB, 3, 8, C), f32),
-            V((NB, 8, C), f32), V((NB, 15, 8, C), f32), V((NB, 4, 8, C), f32),
+            V((2, 32, 3 * C), f32), V((2, 32, 3 * C), f32), V((2, 4, 8, 3 * C), f32), V((2, 3, 8, 3 * C), f32),
+            V((2, 8, 3 * C), f32), V((2, 15, 8, 3 * C), f32), V((2, 4, 8, 3 * C), f32),
             V((8, D), f32), V((16, 128), f32), V((16, 128), f32), V((15, 16, 128), f32),
             V((16, 128), f32), V((3, 16, 128), f32), V((16, 128), f32),
             DMA((2,)), DMA((NB,)), DMA((NB, 2)), DMA((NB, 3)), DMA((NB, 3)), DMA((NB, 4)), DMA((NB, 4)),
             DMA((2,)), DMA((NB,)), DMA((2, 3)), DMA((NB, 3)), DMA((2, 15)), DMA((NB, 15)),
             DMA((NB, 15)), DMA((NB, 15)), DMA((NB,)),
-            DMA((NB,)), DMA((NB,)), DMA((NB, 3)), DMA((NB, 3)), DMA((NB, 15)), DMA((NB, 15)),
-            DMA((NB, 3)), DMA((NB, 3)), DMA((19,)), DMA((19,)),
+            DMA((2,)), DMA((2,)), DMA((2, 3)), DMA((2, 3)), DMA((2, 15)), DMA((2, 15)),
+            DMA((2, 3)), DMA((2, 3)), DMA((19,)), DMA((19,)),
         ],
         compiler_params=pltpu.CompilerParams(collective_id=0, has_side_effects=True, vmem_limit_bytes=62 << 20),
     )(

time: 149 us -> 141 us (0.946)
  Pallas kernels: 140 us -> 132 us
    pallas_call x1, Pallas kernels: 140 us -> 132 us  [local(): pl.pallas_call(body, out_shape=[jax.ShapeDtypeStruct((N, D), bf16), jax.S...]
where the time goes in v3:
time: 141 us
  Pallas kernels  132 us (94%)
  local copies, waits for them, and re-layouts  5.21 us (4%)
  other arithmetic  3.09 us (2%)
    pallas_call x1, Pallas kernels, local(): pl.pallas_call(body, out_shape=[jax.ShapeDtypeStruct((N, D), bf16), jax.S...  132 us
    unnamed x12, local copies, waits for them, and re-layouts  5.21 us
    convert_element_type x1, other arithmetic, local(): gw.astype(f32)  3.09 us

profile of v3, /device:TPU:0, one launch (start us, length us, event | category | flops | bytes accessed | tf_op | source)
XLA Modules:
  0.0 140.5 jit_solution(12097894808907791970)
XLA Ops:
  0.6 131.6 %shard_map.101 = (bf16[768,1536]{1,0:T(8,128)(2,1)}, bf16[768,1536]{1,0:T(8,128)(2,1)}, bf16[192,3072]{1,0:T(8,128)(2,1)}, f32[31,1536]{1,0:T(8,128)}, f32[12,128]{1,0:T(8,128)}) custom-call(bf16[768,1536]{1,0:T(8,128)(2,1)} %bitcast.9, bf16[768,1536]{1,0:T(8,128)(2,1)} %bitcast.10, bf16[192,3072]{1,0:T(8,128)(2,1)} %w.1, f32[31,1536]{1,0:T(8,128)} %kern.1, ...), custom_call_target="tpu_custom_call" | custom-call | tf_op jit(solution)/shard_map/pallas_call | solution.py:565
  132.2 0.0 copy-start.1
  132.2 3.1 %convert_element_type.3 = f32[192,3072]{1,0:T(8,128)} convert(bf16[192,3072]{1,0:T(8,128)(2,1)} %get-tuple-element.12) | non-fusion elementwise | flops 589824 | bytes 3538944 | tf_op jit(solution)/shard_map/convert_element_type | solution.py:604
  135.3 0.0 copy-done.1
  135.3 0.0 copy-start
  135.3 1.4 %copy.15 = bf16[16,48,1536]{2,1,0:T(8,128)(2,1)} copy(bf16[16,48,1536]{2,1,0:T(8,128)(2,1)S(1)} %bitcast.8) | data formatting | bytes 4718592
  136.7 1.1 copy-done
  137.8 0.0 copy-start.2
  137.8 0.0 copy-start.3
  137.8 1.4 copy.16
  139.2 0.0 copy-done.2
  139.2 0.7 copy.17
  139.9 0.0 copy-done.3
  139.9 0.6 copy.18
Async XLA Ops:
  132.2 3.1 %copy-start.1 = (bf16[768,1536]{1,0:T(8,128)(2,1)S(1)}, bf16[768,1536]{1,0:T(8,128)(2,1)}, u32[]{:S(2)}) copy-start(bf16[768,1536]{1,0:T(8,128)(2,1)} %get-tuple-element.10) | copy-start | bytes 7077892
  135.3 2.5 %copy-start = (bf16[768,1536]{1,0:T(8,128)(2,1)S(1)}, bf16[768,1536]{1,0:T(8,128)(2,1)}, u32[]{:S(2)}) copy-start(bf16[768,1536]{1,0:T(8,128)(2,1)} %get-tuple-element.11) | copy-start | bytes 7077892
  137.8 1.4 %copy-start.2 = (f32[31,1536]{1,0:T(8,128)S(1)}, f32[31,1536]{1,0:T(8,128)}, u32[]{:S(2)}) copy-start(f32[31,1536]{1,0:T(8,128)} %get-tuple-element.23) | copy-start | bytes 571396
  137.8 2.1 %copy-start.3 = (f32[12,128]{1,0:T(8,128)S(1)}, f32[12,128]{1,0:T(8,128)}, u32[]{:S(2)}) copy-start(f32[12,128]{1,0:T(8,128)} %get-tuple-element.14) | copy-start | bytes 18436

commit v4 on v3

--- a/solution.py
+++ b/solution.py
@@ -37,7 +37,7 @@
 def body(
     frames, cot, w, kern, gain, lens,
     mo_o, fg_o, gw_o, gk_o, gg_o,
-    nat0, nat1, pm, pmt, fr, up, mean, istd, sc, sct, W, gh, h, glu, gcp, mot, kg, len16, gs,
+    nat0, nat1, pm, pmt, fr, up, mean, istd, sc, sct, W, gh, h, glu, gcp, kg, len16, gs,
     own, sibs, sibr, s1s, s1r, s2s, s2r, gwp,
     kgl, kgsr, kg1, kg1r, kg2, kg2r, kgo, ggl, ggr, gg2, gg2r, gg3, gg3r, gg4,
     in_sem, mo_sem, wl_sem, wz_s, wz_r, ws_s, ws_r,
@@ -346,6 +346,14 @@
 
         h[...] = jnp.dot(sc[...], W[b].reshape(D, C2), preferred_element_type=f32)
 
+        @pl.when(b >= 4)
+        def _():
+            stage3(b - 4)
+
+        @pl.when(b >= 3)
+        def _():
+            stage2(b - 3)
+
         @pl.when(b >= 1)
         def _():
             stage1(b - 1)
@@ -375,7 +383,7 @@
                 s = sigmoid(acc)
                 swish = acc * s
                 out = jnp.where(live(t0, T, 128), fr[rows, cl].astype(f32).reshape(T, U, 128) + swish, 0.0)
-                mot[rows, vl] = out.reshape(T * U, 128).astype(bf16)
+                nat0[rows, cl] = out.reshape(T * U, 128).astype(bf16)
                 gc = up[rows, cl].astype(f32).reshape(T, U, 128) * (s + swish * (1.0 - s))
                 gcp[lt, pl.ds(t0 + R, T)] = gc
                 for k in taps:
@@ -416,28 +424,16 @@
             ksib(b).start()
 
         own[...] = jnp.dot(sct[: 4 * RB, :], gh[b], preferred_element_type=f32).reshape(4, RB, C2)
-
-        @pl.when(b >= 3)
-        def _():
-            stage3(b - 3)
-
-        @pl.when(b >= 2)
-        def _():
-            stage2(b - 2)
-
-        cols = aligned(b * C, C)
-
-        nat0[:, cols] = jnp.dot(pmt[...], mot[...], preferred_element_type=f32).astype(bf16)
-        mo_copy(b).start()
-        return 0
-
-    def mo_copy(b):
-        cols = aligned(b * C, C)
-        return pltpu.make_async_copy(nat0.at[:, cols], mo_o.at[:, cols], mo_sem.at[b])
+        return 0
 
     lax.fori_loop(0, NB, block, 0)
 
+    stage2(NB - 3)
     stage1(NB - 1)
+    sc[...] = jnp.dot(pmt[...], nat0[...], preferred_element_type=f32).astype(bf16)
+    mo_copy = pltpu.make_async_copy(sc, mo_o, mo_sem.at[0])
+    mo_copy.start()
+    stage3(NB - 4)
     stage2(NB - 2)
     ggl[...] = jnp.zeros_like(ggl)
 
@@ -495,7 +491,7 @@
             gg2[...] = gg3[...] + ggr[...]
             loop15(lambda i: g2(i).start())
 
-        @pl.when(j == 5)
+        @pl.when(j == 0)
         def _():
             stage2(NB - 1)
 
@@ -512,11 +508,7 @@
 
     lax.fori_loop(0, N // NR, ln, 0)
 
-    def mo_done(b, _):
-        mo_copy(b).wait()
-        return 0
-
-    lax.fori_loop(0, NB, mo_done, 0)
+    stage3(NB - 1)
     nat0[...] = jnp.dot(pmt[...], nat1[...], preferred_element_type=f32).astype(bf16)
     fg_copy = pltpu.make_async_copy(nat0, fg_o, in_sem.at[0])
     fg_copy.start()
@@ -527,7 +519,6 @@
     gg4[...] = t
     for j in (1, 2, 3):
         g3(j).start()
-    stage3(NB - 1)
 
     def done(b, _):
         loop15(lambda i: s3(b, i).wait())
@@ -556,6 +547,7 @@
         g3(j).wait()
     gg_o[...] = ((gg4[...] + gg3r[0] + gg3r[1] + gg3r[2]) * root)[0 : D // 128]
     fg_copy.wait()
+    mo_copy.wait()
 
 
 def local(frames, cotangent, w_in, kernel, gain, lengths):
@@ -577,7 +569,7 @@
             V((N, D), bf16), V((N, D), bf16), V((N, N), bf16), V((N, N), bf16), V((N, D), bf16), V((N, D), bf16),
             V((N, 1), f32), V((N, 1), f32), V((N, D), bf16), V((D, N), bf16),
             V((NB, 8, RB, C2), bf16), V((NB, N, C2), bf16), V((N, C2), f32),
-            V((LT, L + 2 * R, U, 128), f32), V((LT, L + 2 * R, U, 128), f32), V((N, C), bf16),
+            V((LT, L + 2 * R, U, 128), f32), V((LT, L + 2 * R, U, 128), f32),
             V((K + 1, 8, 128), f32), V((U, 128), jnp.int32), V((N, D), f32),
             V((4, RB, C2), f32), V((2, 4, RB, C2), bf16), V((NB, 4, RB, C2), bf16),
             V((2, 4, 4, RX, C2), bf16), V((NB, 3, 4, RX, C2), bf16),
@@ -586,7 +578,7 @@
             V((2, 8, 3 * C), f32), V((2, 15, 8, 3 * C), f32), V((2, 4, 8, 3 * C), f32),
             V((8, D), f32), V((16, 128), f32), V((16, 128), f32), V((15, 16, 128), f32),
             V((16, 128), f32), V((3, 16, 128), f32), V((16, 128), f32),
-            DMA((2,)), DMA((NB,)), DMA((NB, 2)), DMA((NB, 3)), DMA((NB, 3)), DMA((NB, 4)), DMA((NB, 4)),
+            DMA((2,)), DMA((1,)), DMA((NB, 2)), DMA((NB, 3)), DMA((NB, 3)), DMA((NB, 4)), DMA((NB, 4)),
             DMA((2,)), DMA((NB,)), DMA((2, 3)), DMA((NB, 3)), DMA((2, 15)), DMA((NB, 15)),
             DMA((NB, 15)), DMA((NB, 15)), DMA((NB,)),
             DMA((2,)), DMA((2,)), DMA((2, 3)), DMA((2, 3)), DMA((2, 15)), DMA((2, 15)),

time: 141 us -> 137 us (0.972)
  Pallas kernels: 132 us -> 128 us
    pallas_call x1, Pallas kernels: 132 us -> 128 us  [local(): pl.pallas_call(body, out_shape=[jax.ShapeDtypeStruct((N, D), bf16), jax.S...]
where the time goes in v4:
time: 137 us
  Pallas kernels  128 us (93%)
  local copies, waits for them, and re-layouts  5.21 us (4%)
  other arithmetic  3.09 us (2%)
    pallas_call x1, Pallas kernels, local(): pl.pallas_call(body, out_shape=[jax.ShapeDtypeStruct((N, D), bf16), jax.S...  128 us
    unnamed x12, local copies, waits for them, and re-layouts  5.21 us
    convert_element_type x1, other arithmetic, local(): gw.astype(f32)  3.09 us

profile of v4, /device:TPU:0, one launch (start us, length us, event | category | flops | bytes accessed | tf_op | source)
XLA Modules:
  0.0 137.0 jit_solution(4570710532765275485)
XLA Ops:
  0.6 128.1 %shard_map.101 = (bf16[768,1536]{1,0:T(8,128)(2,1)}, bf16[768,1536]{1,0:T(8,128)(2,1)}, bf16[192,3072]{1,0:T(8,128)(2,1)}, f32[31,1536]{1,0:T(8,128)}, f32[12,128]{1,0:T(8,128)}) custom-call(bf16[768,1536]{1,0:T(8,128)(2,1)} %bitcast.9, bf16[768,1536]{1,0:T(8,128)(2,1)} %bitcast.10, bf16[192,3072]{1,0:T(8,128)(2,1)} %w.1, f32[31,1536]{1,0:T(8,128)} %kern.1, ...), custom_call_target="tpu_custom_call" | custom-call | tf_op jit(solution)/shard_map/pallas_call | solution.py:557
  128.7 0.0 copy-start.1
  128.7 3.1 %convert_element_type.3 = f32[192,3072]{1,0:T(8,128)} convert(bf16[192,3072]{1,0:T(8,128)(2,1)} %get-tuple-element.12) | non-fusion elementwise | flops 589824 | bytes 3538944 | tf_op jit(solution)/shard_map/convert_element_type | solution.py:596
  131.8 0.0 copy-done.1
  131.8 0.0 copy-start
  131.8 1.4 %copy.15 = bf16[16,48,1536]{2,1,0:T(8,128)(2,1)} copy(bf16[16,48,1536]{2,1,0:T(8,128)(2,1)S(1)} %bitcast.8) | data formatting | bytes 4718592
  133.2 1.1 copy-done
  134.3 0.0 copy-start.2
  134.3 0.0 copy-start.3
  134.3 1.4 %copy.16 = bf16[16,48,1536]{2,1,0:T(8,128)(2,1)} copy(bf16[16,48,1536]{2,1,0:T(8,128)(2,1)S(1)} %bitcast.7) | data formatting | bytes 4718592
  135.7 0.0 copy-done.2
  135.7 0.7 copy.17
  136.4 0.0 copy-done.3
  136.4 0.6 copy.18
Async XLA Ops:
  128.7 3.1 %copy-start.1 = (bf16[768,1536]{1,0:T(8,128)(2,1)S(1)}, bf16[768,1536]{1,0:T(8,128)(2,1)}, u32[]{:S(2)}) copy-start(bf16[768,1536]{1,0:T(8,128)(2,1)} %get-tuple-element.10) | copy-start | bytes 7077892
  131.8 2.5 %copy-start = (bf16[768,1536]{1,0:T(8,128)(2,1)S(1)}, bf16[768,1536]{1,0:T(8,128)(2,1)}, u32[]{:S(2)}) copy-start(bf16[768,1536]{1,0:T(8,128)(2,1)} %get-tuple-element.11) | copy-start | bytes 7077892
  134.3 1.4 %copy-start.2 = (f32[31,1536]{1,0:T(8,128)S(1)}, f32[31,1536]{1,0:T(8,128)}, u32[]{:S(2)}) copy-start(f32[31,1536]{1,0:T(8,128)} %get-tuple-element.23) | copy-start | bytes 571396
  134.3 2.1 %copy-start.3 = (f32[12,128]{1,0:T(8,128)S(1)}, f32[12,128]{1,0:T(8,128)}, u32[]{:S(2)}) copy-start(f32[12,128]{1,0:T(8,128)} %get-tuple-element.14) | copy-start | bytes 18436

commit v5 on v4

--- a/solution.py
+++ b/solution.py
@@ -491,7 +491,7 @@
             gg2[...] = gg3[...] + ggr[...]
             loop15(lambda i: g2(i).start())
 
-        @pl.when(j == 0)
+        @pl.when(j == 4)
         def _():
             stage2(NB - 1)
 
@@ -508,10 +508,10 @@
 
     lax.fori_loop(0, N // NR, ln, 0)
 
-    stage3(NB - 1)
     nat0[...] = jnp.dot(pmt[...], nat1[...], preferred_element_type=f32).astype(bf16)
     fg_copy = pltpu.make_async_copy(nat0, fg_o, in_sem.at[0])
     fg_copy.start()
+    stage3(NB - 1)
     loop15(lambda i: g2(i).wait_recv())
     t = gg2[...]
     for i in range(15):

time: 137 us -> 138 us (level)
  no operation moved by 1% of the time
where the time goes in v5:
time: 138 us; the launch traced here: 137 us
  Pallas kernels  128 us (93%)
  local copies, waits for them, and re-layouts  5.21 us (4%)
  other arithmetic  3.09 us (2%)
    pallas_call x1, Pallas kernels, local(): pl.pallas_call(body, out_shape=[jax.ShapeDtypeStruct((N, D), bf16), jax.S...  128 us
    unnamed x12, local copies, waits for them, and re-layouts  5.21 us
    convert_element_type x1, other arithmetic, local(): gw.astype(f32)  3.09 us

profile of v5, /device:TPU:0, one launch (start us, length us, event | category | flops | bytes accessed | tf_op | source)
XLA Modules:
  0.0 137.4 jit_solution(18317385737976073720)
XLA Ops:
  0.6 128.5 %shard_map.101 = (bf16[768,1536]{1,0:T(8,128)(2,1)}, bf16[768,1536]{1,0:T(8,128)(2,1)}, bf16[192,3072]{1,0:T(8,128)(2,1)}, f32[31,1536]{1,0:T(8,128)}, f32[12,128]{1,0:T(8,128)}) custom-call(bf16[768,1536]{1,0:T(8,128)(2,1)} %bitcast.9, bf16[768,1536]{1,0:T(8,128)(2,1)} %bitcast.10, bf16[192,3072]{1,0:T(8,128)(2,1)} %w.1, f32[31,1536]{1,0:T(8,128)} %kern.1, ...), custom_call_target="tpu_custom_call" | custom-call | tf_op jit(solution)/shard_map/pallas_call | solution.py:557
  129.1 0.0 copy-start.1
  129.1 3.1 %convert_element_type.3 = f32[192,3072]{1,0:T(8,128)} convert(bf16[192,3072]{1,0:T(8,128)(2,1)} %get-tuple-element.12) | non-fusion elementwise | flops 589824 | bytes 3538944 | tf_op jit(solution)/shard_map/convert_element_type | solution.py:596
  132.2 0.0 copy-done.1
  132.2 0.0 copy-start
  132.2 1.4 %copy.15 = bf16[16,48,1536]{2,1,0:T(8,128)(2,1)} copy(bf16[16,48,1536]{2,1,0:T(8,128)(2,1)S(1)} %bitcast.8) | data formatting | bytes 4718592
  133.6 1.1 copy-done
  134.7 0.0 copy-start.2
  134.7 0.0 copy-start.3
  134.7 1.4 %copy.16 = bf16[16,48,1536]{2,1,0:T(8,128)(2,1)} copy(bf16[16,48,1536]{2,1,0:T(8,128)(2,1)S(1)} %bitcast.7) | data formatting | bytes 4718592
  136.1 0.0 copy-done.2
  136.2 0.7 copy.17
  136.8 0.0 copy-done.3
  136.8 0.6 copy.18
Async XLA Ops:
  129.1 3.1 %copy-start.1 = (bf16[768,1536]{1,0:T(8,128)(2,1)S(1)}, bf16[768,1536]{1,0:T(8,128)(2,1)}, u32[]{:S(2)}) copy-start(bf16[768,1536]{1,0:T(8,128)(2,1)} %get-tuple-element.10) | copy-start | bytes 7077892
  132.2 2.5 %copy-start = (bf16[768,1536]{1,0:T(8,128)(2,1)S(1)}, bf16[768,1536]{1,0:T(8,128)(2,1)}, u32[]{:S(2)}) copy-start(bf16[768,1536]{1,0:T(8,128)(2,1)} %get-tuple-element.11) | copy-start | bytes 7077892
  134.7 1.4 %copy-start.2 = (f32[31,1536]{1,0:T(8,128)S(1)}, f32[31,1536]{1,0:T(8,128)}, u32[]{:S(2)}) copy-start(f32[31,1536]{1,0:T(8,128)} %get-tuple-element.23) | copy-start | bytes 571396
  134.7 2.1 %copy-start.3 = (f32[12,128]{1,0:T(8,128)S(1)}, f32[12,128]{1,0:T(8,128)}, u32[]{:S(2)}) copy-start(f32[12,128]{1,0:T(8,128)} %get-tuple-element.14) | copy-start | bytes 18436
